TPU v7x, 128 devices: a whole 4x4x4 slice. The times are simulated.
128 devices in a mesh: rows: 128 (over y, z, x, core).
Axes of the slice: x: 4, y: 4, z: 4, core: 2. Of those that a mesh axis runs over, the one named last changes fastest.
Arguments:
- users: float32 [262144, 128], P('rows'), may hold values from -2.5 to 2.5
- items: float32 [65536, 128], P('rows'), may hold values from -2.5 to 2.5
- ratings: bfloat16 [8192, 2, 256, 256], P('rows'), may hold values from -6 to 6
- observed: int32 [8192, 2, 8192], P('rows'), may hold values from 0 to 255
- tile_user: int32 [8192, 2], P('rows'), may hold values from 0 to 7
- fetch_owner: int32 [8192, 1], P('rows'), may hold values from 0 to 127, as said below
- fetch_block: int32 [8192], P('rows'), may hold values from 0 to 1
Outputs:
- new_users: float32 [262144, 128], P('rows')
- new_items: float32 [65536, 128], P('rows')
Inputs may be any that keep to these rules, and one draw needn't show every extreme that they name: `fetch_owner`: within the 64 fetches of one device (aligned blocks of rows), no owner is named more than 1 times, and every device names some owner 1 times.
All inputs are finite; a program needn't handle non-finite values.
Results may differ from a plain program's by a relative error of at most 0.0041.
Values may be sent and summed in bfloat16 or wider, within the bound.
A program may use at most 256 MiB of HBM per device.

v0:
```python
import jax
import jax.numpy as jnp
from jax import lax
from jax.sharding import PartitionSpec as P

LEARN_RATE = 0.02


def unpack_bits(packed_pattern, width):
    shifts = jnp.arange(8, dtype=jnp.int32)
    leading = packed_pattern.shape[:-1]
    bits = jnp.right_shift(packed_pattern.reshape(leading + (width, width // 8, 1)), shifts) & 1
    return bits.reshape(leading + (width, width))


def body(users, items, ratings, observed, tile_user, fetch_owner, fetch_block):
    device_list = lax.axis_size("rows")
    fetches = ratings.shape[0]
    width = ratings.shape[2]
    factors = users.shape[1]
    capacity = (fetches + device_list - 1) // device_list
    owners = fetch_owner[:, 0]
    ordinal = jnp.arange(fetches, dtype=jnp.int32)
    earlier = (owners[None, :] == owners[:, None]) & (ordinal[None, :] < ordinal[:, None])
    placing = jnp.sum(earlier.astype(jnp.int32), axis=1)
    slot_index = owners * capacity + placing
    request_entry = (
        jnp.full((device_list * capacity,), -1, jnp.int32).at[slot_index].set(fetch_block)
    )
    wanted = lax.all_to_all(request_entry, "rows", split_axis=0, concat_axis=0, tiled=True)
    item_blocks = items.astype(jnp.bfloat16).reshape(-1, width, factors)
    local_count = item_blocks.shape[0]
    served = jnp.take(item_blocks, jnp.maximum(wanted, 0), axis=0)
    replies = lax.all_to_all(served, "rows", split_axis=0, concat_axis=0, tiled=True)
    fetched = jnp.take(replies, slot_index, axis=0)
    user_blocks = users.astype(jnp.bfloat16).reshape(-1, width, factors)
    chosen = jnp.take(user_blocks, tile_user, axis=0)
    mask_values = unpack_bits(observed, width).astype(jnp.float32)
    predicted = jnp.einsum("ftir,fjr->ftij", chosen, fetched, preferred_element_type=jnp.float32)
    errors = (mask_values * (predicted - ratings.astype(jnp.float32))).astype(jnp.bfloat16)
    partial_value = jnp.einsum(
        "ftij,ftir->fjr", errors, chosen, preferred_element_type=jnp.float32
    ).astype(jnp.bfloat16)
    outgoing = (
        jnp.zeros((device_list * capacity, width, factors), jnp.bfloat16)
        .at[slot_index]
        .set(partial_value)
    )
    returned_gradient = lax.all_to_all(outgoing, "rows", split_axis=0, concat_axis=0, tiled=True)
    terms = jnp.einsum("ftij,fjr->ftir", errors, fetched, preferred_element_type=jnp.float32)
    member = (tile_user[..., None] == jnp.arange(user_blocks.shape[0], dtype=jnp.int32)).astype(
        jnp.float32
    )
    user_grad = jnp.einsum("ftir,ftu->uir", terms, member, precision=lax.Precision.HIGHEST)
    block_selector = (wanted[:, None] == jnp.arange(local_count, dtype=jnp.int32)[None, :]).astype(
        jnp.bfloat16
    )
    item_factor_gradient = jnp.einsum(
        "ty,tzu->yzu", block_selector, returned_gradient, preferred_element_type=jnp.float32
    )
    new_users = users - LEARN_RATE * user_grad.reshape(users.shape)
    new_items = items - LEARN_RATE * item_factor_gradient.reshape(items.shape)
    return (new_users, new_items)


def solution(mesh):
    placed = (
        P("rows", None),
        P("rows", None),
        P("rows", None, None, None),
        P("rows", None, None),
        P("rows", None),
        P("rows", None),
        P("rows"),
    )
    return jax.shard_map(
        body,
        mesh=mesh,
        in_specs=placed,
        out_specs=(P("rows", None), P("rows", None)),
        check_vma=False,
    )
```

profile of v0, /device:TPU:0, one launch (start us, length us, event | category | flops | bytes accessed | tf_op | source)
XLA Modules:
  0.0 336.8 jit_solution(12386465390858054596)
XLA Ops:
  0.6 0.9 convert_reduce_fusion
  1.5 0.7 and_bitcast_fusion
  2.2 0.9 scatter_custom_fusion
  3.1 0.7 copy.46
  3.9 11.1 %all-to-all-start = ((s32[128,1,1]{2,1,0:T(1,128)}), s32[128,1,1]{2,1,0:T(1,128)S(1)}, u32[]{:S(2)}, u32[]{:S(2)}) async-start(s32[128,1,1]{2,1,0:T(1,128)} %copy.46), calls=%async_computation | async-start | bytes 131072 | tf_op jit(solution)/shard_map/all_to_all | solution.py:30
  15.0 1.0 convert_element_type.26
  16.0 8.2 %all-to-all-done = s32[128,1,1]{2,1,0:T(1,128)S(1)} async-done(((s32[128,1,1]{2,1,0:T(1,128)}), s32[128,1,1]{2,1,0:T(1,128)S(1)}, u32[]{:S(2)}, u32[]{:S(2)}) %all-to-all-start) | async-done | bytes 544 | tf_op jit(solution)/shard_map/all_to_all | solution.py:30
  24.2 4.7 %fusion.32 = (s32[128]{0:T(128)S(1)}, s32[128]{0:T(128)S(1)}) fusion(s32[128,1,1]{2,1,0:T(1,128)S(1)} %all-to-all-done), kind=kLoop, calls=%fused_computation.51 | loop fusion | flops 128 | bytes 1536 | tf_op jit(solution)/shard_map/all_to_all | solution.py:30
  28.9 6.5 %gather_fusion.1 = bf16[128,256,128]{2,1,0:T(8,128)(2,1)} fusion(bf16[2,256,128]{2,1,0:T(8,128)(2,1)S(1)} %bitcast.43, s32[1024]{0:T(1024)S(1)} %pad_clamp_fusion.1), kind=kCustom, calls=%fused_computation.1 | custom fusion | bytes 16777728 | tf_op jit(solution)/shard_map/jit(_take)/gather | solution.py:33
  35.4 7.5 %broadcast_select_fusion = bf16[128,256,128]{2,1,0:T(8,128)(2,1)} fusion(bf16[128,256,128]{2,1,0:T(8,128)(2,1)} %gather_fusion.1, pred[128]{0:T(512)(128)(4,1)S(1)} %maximum_compare_fusion), kind=kLoop, calls=%fused_computation.12 | loop fusion | flops 4194304 | bytes 16777344 | tf_op jit(solution)/shard_map/jit(_take)/select_n | solution.py:33
  42.9 6.1 %all-to-all-start.1 = ((bf16[128,256,128]{2,1,0:T(8,128)(2,1)}), bf16[128,256,128]{2,1,0:T(8,128)(2,1)}, u32[]{:S(2)}, u32[]{:S(2)}) async-start(bf16[128,256,128]{2,1,0:T(8,128)(2,1)} %broadcast_select_fusion), calls=%async_computation.1 | async-start | bytes 16777216 | tf_op jit(solution)/shard_map/all_to_all | solution.py:34
  49.0 8.3 %copy.41 = s32[64,2,8192]{0,2,1:T(8,128)} copy(s32[64,2,8192]{2,1,0:T(2,128)} %param.10) | data formatting | bytes 8388608 | tf_op args[3]
  57.3 8.7 %copy.42 = s32[64,2,256,32]{2,3,1,0:T(8,128)} copy(s32[64,2,256,32]{0,3,2,1:T(8,128)} %bitcast.47) | data formatting | bytes 8388608 | tf_op jit(solution)/shard_map/shift_right_arithmetic | solution.py:12
  66.0 12.8 %broadcast_bitcast_fusion = s32[64,2,256,256]{2,3,1,0:T(8,128)} fusion(s32[64,2,256,32]{2,3,1,0:T(8,128)} %copy.42), kind=kLoop, calls=%fused_computation.8 | loop fusion | bytes 37748736 | tf_op jit(solution)/shard_map/shift_right_arithmetic | solution.py:12
  78.8 0.0 copy-start
  78.9 0.0 copy-start.2
  78.9 33.5 %copy.43 = s32[64,2,256,256]{3,2,1,0:T(8,128)} copy(s32[64,2,256,256]{2,3,1,0:T(8,128)} %broadcast_bitcast_fusion) | data formatting | bytes 67108864 | tf_op jit(solution)/shard_map/shift_right_arithmetic | solution.py:12
  112.4 0.1 shift_right_arithmetic.26
  112.5 0.0 copy-done
  112.5 0.1 convert_element_type.24
  112.6 0.0 copy-done.2
  112.6 0.1 copy.45
  112.7 0.1 reshape.60
  112.8 0.1 copy.44
  112.9 6.5 %gather_fusion = bf16[128,256,128]{2,1,0:T(8,128)(2,1)} fusion(bf16[8,256,128]{2,1,0:T(8,128)(2,1)S(1)} %bitcast.44, s32[1024]{0:T(1024)S(1)} %pad_clamp_fusion.2), kind=kCustom, calls=%fused_computation | custom fusion | bytes 16777728 | tf_op jit(solution)/shard_map/jit(_take)/gather | solution.py:37
  119.5 29.8 %all-to-all-done.1 = bf16[128,256,128]{2,1,0:T(8,128)(2,1)} async-done(((bf16[128,256,128]{2,1,0:T(8,128)(2,1)}), bf16[128,256,128]{2,1,0:T(8,128)(2,1)}, u32[]{:S(2)}, u32[]{:S(2)}) %all-to-all-start.1) | async-done | bytes 8388640 | tf_op jit(solution)/shard_map/all_to_all | solution.py:34
  149.3 6.4 %gather_fusion.2 = bf16[64,256,128]{2,1,0:T(8,128)(2,1)} fusion(bf16[128,256,128]{2,1,0:T(8,128)(2,1)} %all-to-all-done.1, s32[1024]{0:T(1024)S(1)} %pad_clamp_fusion), kind=kCustom, calls=%fused_computation.2 | custom fusion | bytes 8388864 | tf_op jit(solution)/shard_map/jit(_take)/gather | solution.py:35
  155.7 27.8 %multiply_convert_fusion = bf16[64,2,256,256]{3,2,1,0:T(8,128)(2,1)} fusion(bf16[64,2,256,256]{3,2,1,0:T(8,128)(2,1)} %param.9, s32[64,2,256,256]{3,2,1,0:T(8,128)} %copy.43, s32[256]{0:T(256)S(1)} %shift_right_arithmetic.26, bf16[64,2,256,128]{3,2,1,0:T(8,128)(2,1)} %bitcast.45, pred[64,2]{1,0:T(8,128)(4,1)S(1)} %copy.44, ...), kind=kOutput, calls=%fused_computation.5 | convolution fusion | flops 2212495360 | bytes 79692992 | tf_op jit(solution)/shard_map/ftir,fjr->ftij/dot_general | solution.py:39
  183.5 13.0 %bitcast_convert_fusion = bf16[64,256,128]{2,1,0:T(8,128)(2,1)} fusion(bf16[64,2,256,256]{3,2,1,0:T(8,128)(2,1)} %multiply_convert_fusion, bf16[64,2,256,128]{3,2,1,0:T(8,128)(2,1)} %bitcast.46, pred[64,2]{1,0:T(8,128)(4,1)S(1)} %copy.44), kind=kOutput, calls=%fused_computation.9 | convolution fusion | flops 2153775104 | bytes 29360256 | tf_op jit(solution)/shard_map/ftij,ftir->fjr/dot_general | solution.py:41
  196.4 5.3 %broadcast_in_dim.55 = bf16[128,256,128]{2,1,0:T(8,128)(2,1)} broadcast(bf16[]{:T(256)} %constant.56.clone.1), dimensions={} | broadcast | bytes 8388610 | tf_op jit(solution)/shard_map/broadcast_in_dim | solution.py:45
  201.7 11.9 %scatter_fusion = bf16[128,256,128]{2,1,0:T(8,128)(2,1)} fusion(bf16[128,256,128]{2,1,0:T(8,128)(2,1)} %broadcast_in_dim.55, s32[64]{0:T(128)S(1)} %bitcast.50, bf16[64,256,128]{2,1,0:T(8,128)(2,1)} %bitcast_convert_fusion), kind=kCustom, calls=%fused_computation.4 | custom fusion | bytes 12583168 | tf_op jit(solution)/shard_map/scatter | solution.py:47
  213.7 13.8 %all-to-all-start.2 = ((bf16[128,256,128]{2,1,0:T(8,128)(2,1)}), bf16[128,256,128]{2,1,0:T(8,128)(2,1)}, u32[]{:S(2)}, u32[]{:S(2)}) async-start(bf16[128,256,128]{2,1,0:T(8,128)(2,1)} %scatter_fusion), calls=%async_computation.2 | async-start | bytes 16777216 | tf_op jit(solution)/shard_map/all_to_all | solution.py:49
  227.4 12.7 %fusion.5 = f32[64,2,256,128]{3,2,1,0:T(8,128)} fusion(bf16[64,2,256,256]{3,2,1,0:T(8,128)(2,1)} %multiply_convert_fusion, bf16[64,256,128]{2,1,0:T(8,128)(2,1)} %gather_fusion.2, pred[64]{0:T(512)(128)(4,1)S(1)} %get-tuple-element.4), kind=kOutput, calls=%fused_computation.15 | convolution fusion | flops 2149580800 | bytes 37748800 | tf_op jit(solution)/shard_map/ftij,fjr->ftir/dot_general | solution.py:50
  240.2 20.1 %fusion.13 = f32[8,256,128]{2,0,1:T(8,128)S(1)} fusion(f32[64,2,256,128]{3,2,1,0:T(8,128)} %fusion.5, s32[64,2]{0,1:T(2,128)S(1)} %copy-done.2), kind=kOutput, calls=%fused_computation.22 | convolution fusion | flops 402916352 | bytes 17826304 | tf_op jit(solution)/shard_map/ftir,ftu->uir/dot_general | solution.py:54
  260.3 0.0 copy-start.1
  260.3 0.2 copy.48
  260.5 1.1 bitcast_subtract_fusion
  261.6 66.5 %all-to-all-done.2 = bf16[128,256,128]{2,1,0:T(8,128)(2,1)} async-done(((bf16[128,256,128]{2,1,0:T(8,128)(2,1)}), bf16[128,256,128]{2,1,0:T(8,128)(2,1)}, u32[]{:S(2)}, u32[]{:S(2)}) %all-to-all-start.2) | async-done | bytes 8388640 | tf_op jit(solution)/shard_map/all_to_all | solution.py:49
  328.1 7.9 %fusion.16 = f32[2,256,128]{2,0,1:T(2,128)S(1)} fusion(bf16[128,256,128]{2,1,0:T(8,128)(2,1)} %all-to-all-done.2, s32[128]{0:T(128)S(1)} %get-tuple-element.2), kind=kOutput, calls=%fused_computation.23 | convolution fusion | flops 16843008 | bytes 8651264 | tf_op jit(solution)/shard_map/ty,tzu->yzu/dot_general | solution.py:58
  336.0 0.0 copy-done.1
  336.1 0.7 bitcast_subtract_fusion.1
  (8 shorter events, 0.1 us)
Async XLA Ops:
  3.9 20.4 %all-to-all-start = ((s32[128,1,1]{2,1,0:T(1,128)}), s32[128,1,1]{2,1,0:T(1,128)S(1)}, u32[]{:S(2)}, u32[]{:S(2)}) async-start(s32[128,1,1]{2,1,0:T(1,128)} %copy.46), calls=%async_computation | async-start | bytes 131072 | tf_op jit(solution)/shard_map/all_to_all | solution.py:30
  42.9 106.4 %all-to-all-start.1 = ((bf16[128,256,128]{2,1,0:T(8,128)(2,1)}), bf16[128,256,128]{2,1,0:T(8,128)(2,1)}, u32[]{:S(2)}, u32[]{:S(2)}) async-start(bf16[128,256,128]{2,1,0:T(8,128)(2,1)} %broadcast_select_fusion), calls=%async_computation.1 | async-start | bytes 16777216 | tf_op jit(solution)/shard_map/all_to_all | solution.py:34
  78.8 33.6 %copy-start = (f32[2048,128]{1,0:T(8,128)S(1)}, f32[2048,128]{1,0:T(8,128)}, u32[]{:S(2)}) copy-start(f32[2048,128]{1,0:T(8,128)} %param.7) | copy-start | bytes 3145732
  78.9 33.7 %copy-start.2 = (s32[64,2]{0,1:T(2,128)S(1)}, s32[64,2]{0,1:T(2,128)}, u32[]{:S(2)}) copy-start(s32[64,2]{0,1:T(2,128)} %param.11) | copy-start | bytes 1540
  213.7 114.4 %all-to-all-start.2 = ((bf16[128,256,128]{2,1,0:T(8,128)(2,1)}), bf16[128,256,128]{2,1,0:T(8,128)(2,1)}, u32[]{:S(2)}, u32[]{:S(2)}) async-start(bf16[128,256,128]{2,1,0:T(8,128)(2,1)} %scatter_fusion), calls=%async_computation.2 | async-start | bytes 16777216 | tf_op jit(solution)/shard_map/all_to_all | solution.py:49
  260.3 75.7 %copy-start.1 = (f32[512,128]{1,0:T(8,128)S(1)}, f32[512,128]{1,0:T(8,128)}, u32[]{:S(2)}) copy-start(f32[512,128]{1,0:T(8,128)} %param.8) | copy-start | bytes 786436
where the time goes:
time: 342 us; the launch traced here: 337 us
  waiting for transfers between devices  105 us (31%)
  local copies, waits for them, and re-layouts  102 us (30%)
  matrix products  81.6 us (24%)
  starting transfers between devices  31 us (9%)
  other arithmetic  16.6 us (5%)
    all_to_all x1, waiting for transfers between devices, body(): lax.all_to_all(outgoing, 'rows', split_axis=0, concat_axis=0, tiled=True)  66.5 us
    shift_right_arithmetic x5, local copies, waits for them, and re-layouts, unpack_bits(): jnp.right_shift(packed_pattern.reshape(leading + (width, width // 8, 1)),...  55.1 us
    all_to_all x1, waiting for transfers between devices, body(): lax.all_to_all(served, 'rows', split_axis=0, concat_axis=0, tiled=True)  29.8 us
    dot_general x1, matrix products, body(): jnp.einsum('ftir,fjr->ftij', chosen, fetched, preferred_element_type=jnp....  27.8 us
    dot_general x1, matrix products, body(): jnp.einsum('ftir,ftu->uir', terms, member, precision=lax.Precision.HIGHEST)  20.1 us
    all_to_all x1, starting transfers between devices, body(): lax.all_to_all(outgoing, 'rows', split_axis=0, concat_axis=0, tiled=True)  13.8 us
    dot_general x1, matrix products, body(): jnp.einsum('ftij,ftir->fjr', errors, chosen, preferred_element_type=jnp.f...  13 us
    dot_general x1, matrix products, body(): jnp.einsum('ftij,fjr->ftir', errors, fetched, preferred_element_type=jnp....  12.7 us
  transfers between devices with their start and end apart: 3, of which 3 were waited for; matrix products, arithmetic and copies ran while one was open for 31% of the time, Pallas kernels for 0%

commit v1 on v0

v1 whole, which is shorter than its diff:
```python
import functools

import jax
import jax.numpy as jnp
from jax import lax
from jax.experimental import pallas as pl
from jax.experimental.pallas import tpu as pltpu
from jax.sharding import PartitionSpec as P

LEARN_RATE = 0.02
MESH = pl.DeviceIdType.MESH
R = 128
BS = 256
FETCHES = 64
ABSENT = 1e30

ORDERS = ((2, 0, 1), (0, 1, 2), (1, 2, 0))
GATHER_ROWS = ((0, 176), (176, 176), (352, 160))
REDUCE_ROWS = ((0, 96), (96, 80), (176, 80))


def position():
    me = lax.axis_index("rows")
    return (me // 32, (me // 8) % 4, (me // 2) % 4, me % 2)


def shifted(where, axis, step):
    y, z, x, core = [
        lax.rem(w + 4 + step, 4) if a == axis else w for a, w in enumerate(where[:3])
    ] + [where[3]]
    return ((y * 4 + z) * 4 + x) * 2 + core


def sibling(where):
    y, z, x, core = where
    return ((y * 4 + z) * 4 + x) * 2 + 1 - core


def greet(where):
    barrier = pltpu.get_barrier_semaphore()
    partners = [shifted(where, a, s) for a in range(3) for s in (1, -1, 2)] + [sibling(where)]
    for partner in partners:
        pl.semaphore_signal(barrier, inc=1, device_id=(partner,), device_id_type=MESH)
    pl.semaphore_wait(barrier, len(partners))


class Sender:
    def __init__(self, send_sems, recv_sems):
        self.send_sems, self.recv_sems, self.copies = send_sems, recv_sems, []

    def send(self, src, dst, device):
        n = len(self.copies)
        copy = pltpu.make_async_remote_copy(
            src_ref=src,
            dst_ref=dst,
            send_sem=self.send_sems.at[n],
            recv_sem=self.recv_sems.at[n],
            device_id=(device,),
            device_id_type=MESH,
        )
        copy.start()
        self.copies.append(copy)
        return copy

    def finish(self):
        for copy in self.copies:
            copy.wait_send()


GATHER_COPIES = 3 * (3 + 2 + 3 + 2 + 6 + 5) + 1 + 3 * (1 + 3 + 10 + 5)


def gather_kernel(
    items, ratings, observed, spread, bits, gathered, masked,
    own, words, rate_in, obs_in, rate_out, in_sems, out_sems, own_sem, send_sems, recv_sems,
):
    where = position()
    core = where[3]
    net = Sender(send_sems, recv_sems)

    def fetch_in(f, slot):
        return (
            pltpu.make_async_copy(ratings.at[f], rate_in.at[slot], in_sems.at[0, slot]),
            pltpu.make_async_copy(observed.at[f], obs_in.at[slot], in_sems.at[1, slot]),
        )

    def fetch_out(f, slot):
        return pltpu.make_async_copy(rate_out.at[slot], masked.at[f], out_sems.at[slot])

    for copy in fetch_in(0, 0):
        copy.start()

    def one(f, carry):
        slot = lax.rem(f, 2)

        @pl.when(f + 1 < FETCHES)
        def _():
            for copy in fetch_in(f + 1, 1 - slot):
                copy.start()

        for copy in fetch_in(f, slot):
            copy.wait()

        @pl.when(f >= 2)
        def _():
            fetch_out(f - 2, slot).wait()

        lane_group = lax.broadcasted_iota(jnp.int32, (64, 128), 1) // 32
        for t in range(2):
            packed = obs_in[slot, pl.ds(t, 64, stride=2), :].astype(jnp.float32)
            for quarter in range(4):
                words[t, pl.ds(quarter, 64, stride=4), :] = jnp.where(
                    lane_group == quarter, packed, 0.0
                )
            wide = jnp.dot(
                words[t].astype(jnp.bfloat16), spread[...], preferred_element_type=jnp.float32
            )
            seen = (wide.astype(jnp.int32) & bits[...]) != 0
            rate_out[slot, t] = jnp.where(
                seen, rate_in[slot, t].astype(jnp.float32), ABSENT
            ).astype(jnp.bfloat16)
        fetch_out(f, slot).start()
        return carry

    def work(first, last):
        lax.fori_loop(first, last, one, 0)

    def part(p, d1, d2, d3):
        a1, a2, a3 = ORDERS[p]
        index = [None] * 3
        index[a1], index[a2], index[a3] = d1, d2, d3
        return gathered.at[(core, *index, pl.ds(*GATHER_ROWS[p]))]

    every = slice(None)
    here = gathered.at[core, 0, 0, 0]
    own[...] = items[...].astype(jnp.bfloat16)
    place = pltpu.make_async_copy(own, here, own_sem)
    place.start()
    greet(where)

    first, line, plane, pair = {}, {}, {}, []
    twin = sibling(where)

    def mirror(p, d1, d2, d3):
        pair.append(net.send(part(p, d1, d2, d3), part(p, d1, d2, d3), twin))

    thirds = range(3)
    for p in thirds:
        a1, a2, a3 = ORDERS[p]
        mine = own.at[pl.ds(*GATHER_ROWS[p])]
        for s in (1, -1, 2):
            first[p, s] = net.send(mine, part(p, -s % 4, 0, 0), shifted(where, a1, s))
    for p in thirds:
        a1, a2, a3 = ORDERS[p]
        mine = own.at[pl.ds(*GATHER_ROWS[p])]
        for s in (1, -1):
            plane[p, 0, s] = net.send(mine, part(p, 0, 0, -s % 4), shifted(where, a3, s))
    pair.append(net.send(own, here, twin))
    place.wait()
    work(0, 4)
    groups = {0: (0, 0), 1: (slice(1, 4), 0), 2: (every, 3), 3: (every, 1), 4: (every, 2)}
    onward = {0: 1, 1: 1, 2: -1, 3: -1, 4: 1}

    def spread_group(p, g):
        a3 = ORDERS[p][2]
        d1, d2 = groups[g]
        for s in (1, -1):
            plane[p, g, s] = net.send(part(p, d1, d2, 0), part(p, d1, d2, -s % 4), shifted(where, a3, s))

    def pass_on(p, g):
        a3 = ORDERS[p][2]
        d1, d2 = groups[g]
        for s in (1, -1):
            plane[p, g, s].wait_recv()
            if onward[g] == s:
                plane[p, g, 2] = net.send(
                    part(p, d1, d2, -s % 4), part(p, d1, d2, 2), shifted(where, a3, s)
                )
            mirror(p, d1, d2, -s % 4)

    for p in thirds:
        a2 = ORDERS[p][1]
        for s in (1, -1, 2):
            first[p, s].wait_recv()
        for s in (1, -1, 2):
            line[p, s] = net.send(part(p, every, 0, 0), part(p, every, -s % 4, 0), shifted(where, a2, s))
    for p in thirds:
        spread_group(p, 1)
        mirror(p, slice(1, 4), 0, 0)
    work(4, 8)
    for p in thirds:
        pass_on(p, 0)
    work(8, 14)
    for g, s in ((2, 1), (3, -1), (4, 2)):
        for p in thirds:
            line[p, s].wait_recv()
            spread_group(p, g)
            mirror(p, every, -s % 4, 0)
        if g == 2:
            for p in thirds:
                pass_on(p, 1)
        work(14 + 6 * (g - 2), 20 + 6 * (g - 2))
    for g, upto in ((2, 42), (3, 52), (4, 64)):
        for p in thirds:
            pass_on(p, g)
        work({2: 32, 3: 42, 4: 52}[g], upto)
    for slot in range(2):
        fetch_out(FETCHES - 2 + slot, slot).wait()
    for g in groups:
        for p in thirds:
            plane[p, g, 2].wait_recv()
            mirror(p, *groups[g], 2)
    for copy in pair:
        copy.wait_recv()
    net.finish()


def gather(items, ratings, observed, spread, bits):
    return pl.pallas_call(
        gather_kernel,
        out_shape=(
            jax.ShapeDtypeStruct((2, 4, 4, 4, 512, R), jnp.bfloat16),
            jax.ShapeDtypeStruct(ratings.shape, jnp.bfloat16),
        ),
        in_specs=[
            pl.BlockSpec(memory_space=pltpu.VMEM),
            pl.BlockSpec(memory_space=pl.ANY),
            pl.BlockSpec(memory_space=pl.ANY),
            pl.BlockSpec(memory_space=pltpu.VMEM),
            pl.BlockSpec(memory_space=pltpu.VMEM),
        ],
        out_specs=[pl.BlockSpec(memory_space=pl.ANY)] * 2,
        scratch_shapes=[
            pltpu.VMEM((512, R), jnp.bfloat16),
            pltpu.VMEM((2, BS, 128), jnp.float32),
            pltpu.VMEM((2, 2, BS, BS), jnp.bfloat16),
            pltpu.VMEM((2, 128, 128), jnp.int32),
            pltpu.VMEM((2, 2, BS, BS), jnp.bfloat16),
            pltpu.SemaphoreType.DMA((2, 2)),
            pltpu.SemaphoreType.DMA((2,)),
            pltpu.SemaphoreType.DMA,
            pltpu.SemaphoreType.DMA((GATHER_COPIES,)),
            pltpu.SemaphoreType.DMA((GATHER_COPIES,)),
        ],
        compiler_params=pltpu.CompilerParams(
            collective_id=0, has_side_effects=True, vmem_limit_bytes=48 << 20
        ),
        name="gather_items",
    )(items, ratings, observed, spread, bits)


def tile_kernel(
    block_of, tile_user, owner, fetch_block, users, masked, fetched, new_users, partial, slots,
    user16, user16t,
):
    f = pl.program_id(0)

    @pl.when(f == 0)
    def _():
        def block(b, carry):
            rows = pl.ds(b * BS, BS)
            value = users[rows, :]
            user16[b] = value.astype(jnp.bfloat16)
            user16t[b] = value.T.astype(jnp.bfloat16)
            new_users[rows, :] = jnp.zeros((BS, R), jnp.float32)
            return carry

        lax.fori_loop(0, 8, block, 0)

        def clear(o, carry):
            slots[o] = -1
            return carry

        lax.fori_loop(0, 128, clear, 0)

        def note(g, carry):
            slots[owner[g]] = g * 2 + fetch_block[g]
            return carry

        lax.fori_loop(0, FETCHES, note, 0)

    item = fetched[0]
    total = jnp.zeros((R, BS), jnp.float32)
    for t in range(2):
        b = tile_user[f * 2 + t]
        predicted = lax.dot_general(
            user16[b], item, (((1,), (1,)), ((), ())), preferred_element_type=jnp.float32
        )
        miss = predicted - masked[0, t].astype(jnp.float32)
        error = jnp.where(miss > -0.5 * ABSENT, miss, 0.0).astype(jnp.bfloat16)
        total += jnp.dot(user16t[b], error, preferred_element_type=jnp.float32)
        rows = pl.ds(pl.multiple_of(b * BS, BS), BS)
        new_users[rows, :] += jnp.dot(error, item, preferred_element_type=jnp.float32)
    partial[0] = total.astype(jnp.bfloat16)

    @pl.when(f == FETCHES - 1)
    def _():
        def block(b, carry):
            rows = pl.ds(b * BS, BS)
            new_users[rows, :] = users[rows, :] - LEARN_RATE * new_users[rows, :]
            return carry

        lax.fori_loop(0, 8, block, 0)


def tiles(block_of, tile_user, owner, fetch_block, users, masked, fetched):
    return pl.pallas_call(
        tile_kernel,
        grid_spec=pltpu.PrefetchScalarGridSpec(
            num_scalar_prefetch=4,
            grid=(FETCHES,),
            in_specs=[
                pl.BlockSpec(users.shape, lambda f, *_: (0, 0)),
                pl.BlockSpec((1, 2, BS, BS), lambda f, *_: (f, 0, 0, 0)),
                pl.BlockSpec((1, BS, R), lambda f, block_of, *_: (block_of[f], 0, 0)),
            ],
            out_specs=[
                pl.BlockSpec(users.shape, lambda f, *_: (0, 0)),
                pl.BlockSpec((1, R, BS), lambda f, *_: (f, 0, 0)),
                pl.BlockSpec(memory_space=pltpu.SMEM),
            ],
            scratch_shapes=[
                pltpu.VMEM((8, BS, R), jnp.bfloat16),
                pltpu.VMEM((8, R, BS), jnp.bfloat16),
            ],
        ),
        out_shape=(
            jax.ShapeDtypeStruct(users.shape, jnp.float32),
            jax.ShapeDtypeStruct((FETCHES, R, BS), jnp.bfloat16),
            jax.ShapeDtypeStruct((128,), jnp.int32),
        ),
        compiler_params=pltpu.CompilerParams(vmem_limit_bytes=48 << 20),
        name="tile_gradients",
    )(block_of, tile_user, owner, fetch_block, users, masked, fetched)


REDUCE_COPIES = 48 + 3 * (4 + 4 + 4 + 3 + 3)


def reduce_kernel(
    slots, partial, items, new_items,
    parts, outgoing0, outgoing1, outgoing2, arriving0, arriving1, arriving2, dense0, dense1, dense2,
    far0, far1, far2, near0, near1, near2, plane0, plane1, plane2, line0, line1, line2,
    row0, row1, row2, unit0, unit1, unit2, grad, load_sem, send_sems, recv_sems,
):
    outgoing, arriving = (outgoing0, outgoing1, outgoing2), (arriving0, arriving1, arriving2)
    dense, far, near = (dense0, dense1, dense2), (far0, far1, far2), (near0, near1, near2)
    plane, line = (plane0, plane1, plane2), (line0, line1, line2)
    row, unit = (row0, row1, row2), (unit0, unit1, unit2)
    where = position()
    core = where[3]
    twin = sibling(where)
    load = pltpu.make_async_copy(partial, parts, load_sem)
    load.start()
    net = Sender(send_sems, recv_sems)
    greet(where)
    load.wait()
    thirds = range(3)

    def fill(target, p, parity, d3, d2):
        a1, a2, a3 = ORDERS[p]
        start, count = REDUCE_ROWS[p]

        def one(d1, carry):
            at = [None] * 3
            at[a1], at[a2], at[a3] = (
                lax.rem(where[a1] + d1, 4), lax.rem(where[a2] + d2, 4), lax.rem(where[a3] + d3, 4)
            )
            code = slots[((at[0] * 4 + at[1]) * 4 + at[2]) * 2 + parity]
            fetch = jnp.maximum(code, 0) // 2
            for block in range(2):
                low, high = max(start, block * R), min(start + count, (block + 1) * R)
                if low < high:
                    keep = (code >= 0) & (lax.rem(jnp.maximum(code, 0), 2) == block)
                    value = parts[fetch, pl.ds(low - block * R, high - low), :]
                    target[d3, d2, d1, pl.ds(low - start, high - low), :] = jnp.where(
                        keep, value, jnp.zeros_like(value)
                    )
            return carry

        lax.fori_loop(0, 4, one, 0)

    pair = {}

    def hand_over(d3, d2):
        for p in thirds:
            fill(outgoing[p], p, 1 - core, d3, d2)
            pair[p, d3, d2] = net.send(
                outgoing[p].at[d3, d2], arriving[p].at[d3, d2], twin
            )

    def collect(d3, d2):
        for p in thirds:
            fill(dense[p], p, core, d3, d2)
            pair[p, d3, d2].wait_recv()
            add_into(dense[p].at[d3, d2], arriving[p].at[d3, d2])

    def add_into(target, other):
        def one(n, carry):
            target[n] = (target[n].astype(jnp.float32) + other[n].astype(jnp.float32)).astype(
                jnp.bfloat16
            )
            return carry

        lax.fori_loop(0, 4, one, 0)

    via = {0: 1, 1: 1, 2: -1, 3: -1}
    relay, direct = {}, {}

    def send_far(d2):
        for p in thirds:
            s = via[d2]
            relay[p, d2] = net.send(
                dense[p].at[2, d2], far[p].at[d2], shifted(where, ORDERS[p][2], s)
            )

    def send_near(d2, s):
        for p in thirds:
            if via[d2] == s:
                relay[p, d2].wait_recv()
                add_into(dense[p].at[s % 4, d2], far[p].at[d2])
            direct[p, d2, s] = net.send(
                dense[p].at[s % 4, d2],
                near[p].at[0 if s == 1 else 1, d2],
                shifted(where, ORDERS[p][2], s),
            )

    todo = [(2, 0), (2, 2), (2, 1), (2, 3), (1, 2), (3, 0), (1, 3), (3, 1)]
    todo += [(1, 0), (3, 2), (1, 1), (3, 3), (0, 0), (0, 1), (0, 2), (0, 3)]
    ahead = 4
    for d3, d2 in todo[:ahead]:
        hand_over(d3, d2)
    for n, (d3, d2) in enumerate(todo):
        collect(d3, d2)
        if d3 == 2:
            send_far(d2)
        elif d3 != 0:
            send_near(d2, 1 if d3 == 1 else -1)
        if n + ahead < len(todo):
            hand_over(*todo[n + ahead])

    for d2 in (2, 1, 3, 0):
        for p in thirds:
            for s in (1, -1):
                direct[p, d2, s].wait_recv()

            def one(n, carry, p=p, d2=d2):
                total = dense[p][0, d2, n].astype(jnp.float32)
                total += near[p][0, d2, n].astype(jnp.float32)
                total += near[p][1, d2, n].astype(jnp.float32)
                plane[p][d2, n] = total.astype(jnp.bfloat16)
                return carry

            lax.fori_loop(0, 4, one, 0)
            if d2 != 0:
                s = {1: 1, 2: 2, 3: -1}[d2]
                direct[p, "line", s] = net.send(
                    plane[p].at[d2], line[p].at[d2 - 1], shifted(where, ORDERS[p][1], s)
                )
    for p in thirds:
        for s in (1, -1, 2):
            direct[p, "line", s].wait_recv()

        def one(n, carry, p=p):
            total = plane[p][0, n].astype(jnp.float32)
            for k in range(3):
                total += line[p][k, n].astype(jnp.float32)
            row[p][n] = total.astype(jnp.bfloat16)
            return carry

        lax.fori_loop(0, 4, one, 0)
        for d1, s in ((1, 1), (2, 2), (3, -1)):
            direct[p, "unit", s] = net.send(
                row[p].at[d1], unit[p].at[d1 - 1], shifted(where, ORDERS[p][0], s)
            )
    for p in thirds:
        start, count = REDUCE_ROWS[p]
        for s in (1, -1, 2):
            direct[p, "unit", s].wait_recv()
        total = row[p][0].astype(jnp.float32)
        for k in range(3):
            total += unit[p][k].astype(jnp.float32)
        grad[pl.ds(start, count), :] = total
    for block in range(2):
        rows = pl.ds(block * BS, BS)
        new_items[rows, :] = items[rows, :] - LEARN_RATE * grad[pl.ds(block * R, R), :].T
    net.finish()


def reduce_items(slots, partial, items):
    def each(*lead):
        return [pltpu.VMEM((*lead, count, BS), jnp.bfloat16) for _, count in REDUCE_ROWS]

    return pl.pallas_call(
        reduce_kernel,
        out_shape=jax.ShapeDtypeStruct(items.shape, jnp.float32),
        in_specs=[
            pl.BlockSpec(memory_space=pltpu.SMEM),
            pl.BlockSpec(memory_space=pl.ANY),
            pl.BlockSpec(memory_space=pltpu.VMEM),
        ],
        out_specs=pl.BlockSpec(memory_space=pltpu.VMEM),
        scratch_shapes=[
            pltpu.VMEM(partial.shape, jnp.bfloat16),
            *each(4, 4, 4),
            *each(4, 4, 4),
            *each(4, 4, 4),
            *each(4, 4),
            *each(2, 4, 4),
            *each(4, 4),
            *each(3, 4),
            *each(4),
            *each(3),
            pltpu.VMEM((BS, BS), jnp.float32),
            pltpu.SemaphoreType.DMA,
            pltpu.SemaphoreType.DMA((REDUCE_COPIES,)),
            pltpu.SemaphoreType.DMA((REDUCE_COPIES,)),
        ],
        compiler_params=pltpu.CompilerParams(
            collective_id=1, has_side_effects=True, vmem_limit_bytes=56 << 20
        ),
        name="reduce_items",
    )(slots, partial, items)


def body(users, items, ratings, observed, tile_user, fetch_owner, fetch_block):
    owner = fetch_owner[:, 0]
    chip = owner // 2
    mine = lax.axis_index("rows") // 2
    away = (
        (chip // 16 - mine // 16) % 4 * 16
        + (chip // 4 % 4 - mine // 4 % 4) % 4 * 4
        + (chip % 4 - mine % 4) % 4
    )
    block_of = ((owner % 2) * 64 + away) * 2 + fetch_block
    word = jnp.arange(128, dtype=jnp.int32)[:, None]
    column = jnp.arange(BS, dtype=jnp.int32)[None, :]
    spread = (word % 32 == column // 8).astype(jnp.bfloat16)
    bits = jnp.broadcast_to(jnp.left_shift(1, column % 8), (BS, BS))
    packed = observed.reshape(FETCHES, 2, 64, 128).transpose(0, 2, 1, 3).reshape(FETCHES, 128, 128)
    gathered, masked = gather(items, ratings, packed, spread, bits)
    new_users, partial, slots = tiles(
        block_of, tile_user.reshape(-1), owner, fetch_block, users, masked,
        gathered.reshape(256, BS, R),
    )
    new_items = reduce_items(slots, partial, items)
    return (new_users, new_items)


def solution(mesh):
    placed = (
        P("rows", None),
        P("rows", None),
        P("rows", None, None, None),
        P("rows", None, None),
        P("rows", None),
        P("rows", None),
        P("rows"),
    )
    return jax.shard_map(
        body,
        mesh=mesh,
        in_specs=placed,
        out_specs=(P("rows", None), P("rows", None)),
        check_vma=False,
    )
```

time: 342 us -> 183 us (0.54)
  Pallas kernels: 0 us -> 171 us
  waiting for transfers between devices: 105 us -> 0 us
  local copies, waits for them, and re-layouts: 102 us -> 8.18 us
  matrix products: 81.6 us -> 0 us
  starting transfers between devices: 31 us -> 0 us
  other arithmetic: 16.6 us -> 0.81 us
    pallas_call x0 -> x3, Pallas kernels: none -> 171 us  [the longest x1 65.7 us: gather(): pl.pallas_call(gather_kernel, out_shape=(jax.ShapeDtypeStruct((2, 4, 4, 4...]
    all_to_all x3 -> x0, waiting for transfers between devices: 105 us -> none  [the longest x1 66.5 us: body(): lax.all_to_all(outgoing, 'rows', split_axis=0, concat_axis=0, tiled=True)]
    dot_general x5 -> x0, matrix products: 81.6 us -> none  [the longest x1 27.8 us: body(): jnp.einsum('ftir,fjr->ftij', chosen, fetched, preferred_element_type=jnp....]
    shift_right_arithmetic x5 -> x0, local copies, waits for them, and re-layouts: 55.1 us -> none  [unpack_bits(): jnp.right_shift(packed_pattern.reshape(leading + (width, width // 8, 1)),...]
    all_to_all x3 -> x0, starting transfers between devices: 31 us -> none  [the longest x1 13.8 us: body(): lax.all_to_all(outgoing, 'rows', split_axis=0, concat_axis=0, tiled=True)]
    gather x3 -> x0, local copies, waits for them, and re-layouts: 19.4 us -> none  [the longest x1 6.52 us: body(): chosen = jnp.take(user_blocks, tile_user, axis=0)]
    scatter x2 -> x0, local copies, waits for them, and re-layouts: 12.8 us -> none  [the longest x1 11.9 us: body(): outgoing = jnp.zeros((device_list * capacity, width, factors), jnp.bfloat...]
    select_n x2, other arithmetic: 7.48 us -> 0.01 us  [body(): spread = (word % 32 == column // 8).astype(jnp.bfloat16)]
  transfers between devices with their start and end apart: 3 -> 0, of which waited for: 3 -> 0; matrix products, arithmetic and copies ran while one was open for 31% -> 0% of each run, Pallas kernels for 0% -> 0%
where the time goes in v1:
time: 183 us; the launch traced here: 181 us
  Pallas kernels  171 us (93%)
  local copies, waits for them, and re-layouts  8.18 us (4%)
    pallas_call x1, Pallas kernels, gather(): pl.pallas_call(gather_kernel, out_shape=(jax.ShapeDtypeStruct((2, 4, 4, 4...  65.7 us
    pallas_call x1, Pallas kernels, tiles(): pl.pallas_call(tile_kernel, grid_spec=pltpu.PrefetchScalarGridSpec(num_sc...  56.1 us
    pallas_call x1, Pallas kernels, reduce_items(): pl.pallas_call(reduce_kernel, out_shape=jax.ShapeDtypeStruct(items.shape,...  49 us
    unnamed x16, local copies, waits for them, and re-layouts  8.02 us

profile of v1, /device:TPU:0, one launch (start us, length us, event | category | flops | bytes accessed | tf_op | source)
XLA Modules:
  0.0 180.5 jit_solution(6993231368491548262)
XLA Ops:
  0.6 0.0 copy-start.4
  0.6 0.0 copy-start.5
  0.7 0.7 multiply_add_fusion.block_of
  1.5 0.8 copy.11
  2.2 0.1 reshape.85.tile_user
  2.4 0.1 compare_convert_fusion.spread
  2.5 0.0 copy-start.1
  2.5 2.2 %copy-done.1 = s32[64,2,8192]{2,1,0:T(2,128)S(1)} copy-done((s32[64,2,8192]{2,1,0:T(2,128)S(1)}, s32[64,2,8192]{2,1,0:T(2,128)}, u32[]{:S(2)}) %copy-start.1) | copy-done | bytes 4194328
  4.7 0.0 copy-start.2
  4.7 0.9 copy-done.2
  5.6 0.0 copy-start.3
  5.6 65.7 %gather_items.1 = (bf16[2,4,4,4,512,128]{5,4,3,2,1,0:T(8,128)(2,1)}, bf16[64,2,256,256]{3,2,1,0:T(8,128)(2,1)}) custom-call(f32[512,128]{1,0:T(8,128)S(1)} %copy-done.2, bf16[64,2,256,256]{3,2,1,0:T(8,128)(2,1)} %ratings.1, s32[64,128,128]{2,1,0:T(8,128)S(1)} %bitcast.8, bf16[128,256]{1,0:T(8,128)(2,1)S(1)} %compare_convert_fusion.spread, ...), custom_call_target="tpu_custom_call" | custom-call | tf_op jit(solution)/shard_map/gather_items/pallas_call | solution.py:219
  71.3 0.0 copy-done.4
  71.3 0.0 copy-done.5
  71.3 0.0 copy-done.3
  71.3 56.1 %tile_gradients.1 = (f32[2048,128]{1,0:T(8,128)}, bf16[64,128,256]{2,1,0:T(8,128)(2,1)S(1)}, s32[128]{0:T(128)S(1)}) custom-call(s32[64]{0:T(128)S(1)} %multiply_add_fusion.block_of, s32[128]{0:T(128)S(1)} %reshape.85.tile_user, s32[64]{0:T(128)S(1)} %bitcast.9, s32[64]{0:T(128)S(1)} %copy-done.4, f32[2048,128]{1,0:T(8,128)S(1)} %copy-done.3, ...), custom_call_target="tpu_custom_call" | custom-call | tf_op jit(solution)/shard_map/tile_gradients/pallas_call | solution.py:307
  127.5 0.0 copy-start
  127.5 1.9 %copy-done = bf16[64,128,256]{2,1,0:T(8,128)(2,1)} copy-done((bf16[64,128,256]{2,1,0:T(8,128)(2,1)}, bf16[64,128,256]{2,1,0:T(8,128)(2,1)S(1)}, u32[]{:S(2)}) %copy-start) | copy-done | bytes 4194328
  129.4 0.0 copy-start.6
  129.4 0.5 copy-done.6
  129.9 49.0 %reduce_items.1 = f32[512,128]{1,0:T(8,128)} custom-call(s32[128]{0:T(128)} %copy-done.6, bf16[64,128,256]{2,1,0:T(8,128)(2,1)} %copy-done, f32[512,128]{1,0:T(8,128)} %items.3), custom_call_target="tpu_custom_call" | custom-call | tf_op jit(solution)/shard_map/reduce_items/pallas_call | solution.py:494
  178.9 1.7 copy.14
  (4 shorter events, 0.0 us)
Async XLA Ops:
  0.6 70.7 %copy-start.4 = (s32[64]{0:T(128)S(1)}, s32[64]{0:T(128)}, u32[]{:S(2)}) copy-start(s32[64]{0:T(128)} %fetch_block.1) | copy-start | bytes 772
  0.6 70.7 %copy-start.5 = (s32[64,1]{0,1:T(1,128)S(1)}, s32[64,1]{0,1:T(1,128)}, u32[]{:S(2)}) copy-start(s32[64,1]{0,1:T(1,128)} %param.12) | copy-start | bytes 772
  2.5 2.2 %copy-start.1 = (s32[64,2,8192]{2,1,0:T(2,128)S(1)}, s32[64,2,8192]{2,1,0:T(2,128)}, u32[]{:S(2)}) copy-start(s32[64,2,8192]{2,1,0:T(2,128)} %param.10) | copy-start | bytes 12582916
  4.7 0.9 copy-start.2
  5.6 65.7 %copy-start.3 = (f32[2048,128]{1,0:T(8,128)S(1)}, f32[2048,128]{1,0:T(8,128)}, u32[]{:S(2)}) copy-start(f32[2048,128]{1,0:T(8,128)} %users.1) | copy-start | bytes 3145732
  127.5 1.9 %copy-start = (bf16[64,128,256]{2,1,0:T(8,128)(2,1)}, bf16[64,128,256]{2,1,0:T(8,128)(2,1)S(1)}, u32[]{:S(2)}) copy-start(bf16[64,128,256]{2,1,0:T(8,128)(2,1)S(1)} %get-tuple-element.11.partial) | copy-start | bytes 12582916
  129.4 0.5 copy-start.6

commit v2 on v1

--- a/solution.py
+++ b/solution.py
@@ -12,6 +12,8 @@
 R = 128
 BS = 256
 FETCHES = 64
+CHUNK = 4
+STEPS = FETCHES // CHUNK
 ABSENT = 1e30
 
 ORDERS = ((2, 0, 1), (0, 1, 2), (1, 2, 0))
@@ -67,59 +69,65 @@
             copy.wait_send()
 
 
-GATHER_COPIES = 3 * (3 + 2 + 3 + 2 + 6 + 5) + 1 + 3 * (1 + 3 + 10 + 5)
+GATHER_COPIES = 3 * (3 + 4 + 12 + 6) + 1 + 3 * (5 + 12 + 6)
 
 
 def gather_kernel(
-    items, ratings, observed, spread, bits, gathered, masked,
-    own, words, rate_in, obs_in, rate_out, in_sems, out_sems, own_sem, send_sems, recv_sems,
+    items, ratings, observed, gathered, masked,
+    spread, wide_own, own, words, rate_in, obs_in, rate_out, in_sems, out_sems, own_sem, send_sems, recv_sems,
 ):
     where = position()
     core = where[3]
     net = Sender(send_sems, recv_sems)
 
-    def fetch_in(f, slot):
+    def fetch_in(n, slot):
+        some = pl.ds(n * CHUNK, CHUNK)
         return (
-            pltpu.make_async_copy(ratings.at[f], rate_in.at[slot], in_sems.at[0, slot]),
-            pltpu.make_async_copy(observed.at[f], obs_in.at[slot], in_sems.at[1, slot]),
+            pltpu.make_async_copy(ratings.at[some], rate_in.at[slot], in_sems.at[0, slot]),
+            pltpu.make_async_copy(observed.at[some], obs_in.at[slot], in_sems.at[1, slot]),
         )
 
-    def fetch_out(f, slot):
-        return pltpu.make_async_copy(rate_out.at[slot], masked.at[f], out_sems.at[slot])
-
-    for copy in fetch_in(0, 0):
-        copy.start()
-
-    def one(f, carry):
-        slot = lax.rem(f, 2)
-
-        @pl.when(f + 1 < FETCHES)
+    def fetch_out(n, slot):
+        return pltpu.make_async_copy(
+            rate_out.at[slot], masked.at[pl.ds(n * CHUNK, CHUNK)], out_sems.at[slot]
+        )
+
+    def one(n, carry):
+        slot = lax.rem(n, 2)
+
+        @pl.when(n + 1 < STEPS)
         def _():
-            for copy in fetch_in(f + 1, 1 - slot):
+            for copy in fetch_in(n + 1, 1 - slot):
                 copy.start()
 
-        for copy in fetch_in(f, slot):
+        for copy in fetch_in(n, slot):
             copy.wait()
 
-        @pl.when(f >= 2)
+        @pl.when(n >= 2)
         def _():
-            fetch_out(f - 2, slot).wait()
+            fetch_out(n - 2, slot).wait()
 
         lane_group = lax.broadcasted_iota(jnp.int32, (64, 128), 1) // 32
-        for t in range(2):
-            packed = obs_in[slot, pl.ds(t, 64, stride=2), :].astype(jnp.float32)
-            for quarter in range(4):
-                words[t, pl.ds(quarter, 64, stride=4), :] = jnp.where(
-                    lane_group == quarter, packed, 0.0
+        bit = jnp.left_shift(1, lax.broadcasted_iota(jnp.int32, (1, BS), 1) % 8)
+
+        def fetch(k, carry):
+            for t in range(2):
+                packed = obs_in[slot, k, pl.ds(t, 64, stride=2), :].astype(jnp.float32)
+                for quarter in range(4):
+                    words[t, pl.ds(quarter, 64, stride=4), :] = jnp.where(
+                        lane_group == quarter, packed, 0.0
+                    )
+                wide = jnp.dot(
+                    words[t].astype(jnp.bfloat16), spread[...], preferred_element_type=jnp.float32
                 )
-            wide = jnp.dot(
-                words[t].astype(jnp.bfloat16), spread[...], preferred_element_type=jnp.float32
-            )
-            seen = (wide.astype(jnp.int32) & bits[...]) != 0
-            rate_out[slot, t] = jnp.where(
-                seen, rate_in[slot, t].astype(jnp.float32), ABSENT
-            ).astype(jnp.bfloat16)
-        fetch_out(f, slot).start()
+                seen = (wide.astype(jnp.int32) & bit) != 0
+                rate_out[slot, k, t] = jnp.where(
+                    seen, rate_in[slot, k, t].astype(jnp.float32), ABSENT
+                ).astype(jnp.bfloat16)
+            return carry
+
+        lax.fori_loop(0, CHUNK, fetch, 0)
+        fetch_out(n, slot).start()
         return carry
 
     def work(first, last):
@@ -133,7 +141,15 @@
 
     every = slice(None)
     here = gathered.at[core, 0, 0, 0]
-    own[...] = items[...].astype(jnp.bfloat16)
+    word = lax.broadcasted_iota(jnp.int32, (128, BS), 0)
+    column = lax.broadcasted_iota(jnp.int32, (128, BS), 1)
+    spread[...] = jnp.where(word % 32 == column // 8, 1.0, 0.0).astype(jnp.bfloat16)
+    read = pltpu.make_async_copy(items, wide_own, own_sem)
+    read.start()
+    for copy in fetch_in(0, 0):
+        copy.start()
+    read.wait()
+    own[...] = wide_own[...].astype(jnp.bfloat16)
     place = pltpu.make_async_copy(own, here, own_sem)
     place.start()
     greet(where)
@@ -157,65 +173,86 @@
             plane[p, 0, s] = net.send(mine, part(p, 0, 0, -s % 4), shifted(where, a3, s))
     pair.append(net.send(own, here, twin))
     place.wait()
-    work(0, 4)
-    groups = {0: (0, 0), 1: (slice(1, 4), 0), 2: (every, 3), 3: (every, 1), 4: (every, 2)}
-    onward = {0: 1, 1: 1, 2: -1, 3: -1, 4: 1}
+    work(0, 1)
+    low, high = slice(0, 2), slice(2, 4)
+    groups = {
+        0: (0, 0), 1: (slice(1, 4), 0), 2: (every, 3), 3: (every, 1), 4: (low, 2), 5: (high, 2)
+    }
+    onward = {0: 1, 1: 1, 2: -1, 3: -1, 4: 1, 5: 1}
 
     def spread_group(p, g):
         a3 = ORDERS[p][2]
         d1, d2 = groups[g]
         for s in (1, -1):
             plane[p, g, s] = net.send(part(p, d1, d2, 0), part(p, d1, d2, -s % 4), shifted(where, a3, s))
-
-    def pass_on(p, g):
-        a3 = ORDERS[p][2]
-        d1, d2 = groups[g]
-        for s in (1, -1):
-            plane[p, g, s].wait_recv()
-            if onward[g] == s:
-                plane[p, g, 2] = net.send(
-                    part(p, d1, d2, -s % 4), part(p, d1, d2, 2), shifted(where, a3, s)
-                )
-            mirror(p, d1, d2, -s % 4)
+        if g > 0:
+            mirror(p, d1, d2, 0)
+
+    def pass_on(g):
+        for p in thirds:
+            a3 = ORDERS[p][2]
+            d1, d2 = groups[g]
+            for s in (1, -1):
+                plane[p, g, s].wait_recv()
+                if onward[g] == s:
+                    plane[p, g, 2] = net.send(
+                        part(p, d1, d2, -s % 4), part(p, d1, d2, 2), shifted(where, a3, s)
+                    )
+                mirror(p, d1, d2, -s % 4)
+
+    def passed(g):
+        for p in thirds:
+            plane[p, g, 2].wait_recv()
+            mirror(p, *groups[g], 2)
 
     for p in thirds:
         a2 = ORDERS[p][1]
         for s in (1, -1, 2):
             first[p, s].wait_recv()
-        for s in (1, -1, 2):
+        for s in (1, -1):
             line[p, s] = net.send(part(p, every, 0, 0), part(p, every, -s % 4, 0), shifted(where, a2, s))
     for p in thirds:
         spread_group(p, 1)
-        mirror(p, slice(1, 4), 0, 0)
-    work(4, 8)
-    for p in thirds:
-        pass_on(p, 0)
-    work(8, 14)
-    for g, s in ((2, 1), (3, -1), (4, 2)):
+    work(1, 2)
+    pass_on(0)
+    work(2, 3)
+    for g, s, half in ((2, 1, low), (3, -1, high)):
         for p in thirds:
             line[p, s].wait_recv()
+            line[p, g + 2] = net.send(
+                part(p, half, -s % 4, 0), part(p, half, 2, 0), shifted(where, ORDERS[p][1], s)
+            )
             spread_group(p, g)
-            mirror(p, every, -s % 4, 0)
-        if g == 2:
-            for p in thirds:
-                pass_on(p, 1)
-        work(14 + 6 * (g - 2), 20 + 6 * (g - 2))
-    for g, upto in ((2, 42), (3, 52), (4, 64)):
-        for p in thirds:
-            pass_on(p, g)
-        work({2: 32, 3: 42, 4: 52}[g], upto)
+    work(3, 5)
+    pass_on(1)
+    work(5, 7)
+    for g, half in ((4, low), (5, high)):
+        for p in thirds:
+            line[p, g].wait_recv()
+            spread_group(p, g)
+    work(7, 9)
+    pass_on(2)
+    passed(0)
+    work(9, 11)
+    pass_on(3)
+    passed(1)
+    work(11, 13)
+    pass_on(4)
+    work(13, 14)
+    pass_on(5)
+    work(14, STEPS)
+    passed(2)
+    passed(3)
     for slot in range(2):
-        fetch_out(FETCHES - 2 + slot, slot).wait()
-    for g in groups:
-        for p in thirds:
-            plane[p, g, 2].wait_recv()
-            mirror(p, *groups[g], 2)
+        fetch_out(STEPS - 2 + slot, slot).wait()
+    passed(4)
+    passed(5)
     for copy in pair:
         copy.wait_recv()
     net.finish()
 
 
-def gather(items, ratings, observed, spread, bits):
+def gather(items, ratings, observed):
     return pl.pallas_call(
         gather_kernel,
         out_shape=(
@@ -223,19 +260,19 @@
             jax.ShapeDtypeStruct(ratings.shape, jnp.bfloat16),
         ),
         in_specs=[
-            pl.BlockSpec(memory_space=pltpu.VMEM),
-            pl.BlockSpec(memory_space=pl.ANY),
-            pl.BlockSpec(memory_space=pl.ANY),
-            pl.BlockSpec(memory_space=pltpu.VMEM),
-            pl.BlockSpec(memory_space=pltpu.VMEM),
+            pl.BlockSpec(memory_space=pltpu.HBM),
+            pl.BlockSpec(memory_space=pltpu.HBM),
+            pl.BlockSpec(memory_space=pltpu.HBM),
         ],
-        out_specs=[pl.BlockSpec(memory_space=pl.ANY)] * 2,
+        out_specs=[pl.BlockSpec(memory_space=pltpu.HBM)] * 2,
         scratch_shapes=[
+            pltpu.VMEM((128, BS), jnp.bfloat16),
+            pltpu.VMEM((512, R), jnp.float32),
             pltpu.VMEM((512, R), jnp.bfloat16),
             pltpu.VMEM((2, BS, 128), jnp.float32),
-            pltpu.VMEM((2, 2, BS, BS), jnp.bfloat16),
-            pltpu.VMEM((2, 128, 128), jnp.int32),
-            pltpu.VMEM((2, 2, BS, BS), jnp.bfloat16),
+            pltpu.VMEM((2, CHUNK, 2, BS, BS), jnp.bfloat16),
+            pltpu.VMEM((2, CHUNK, 128, 128), jnp.int32),
+            pltpu.VMEM((2, CHUNK, 2, BS, BS), jnp.bfloat16),
             pltpu.SemaphoreType.DMA((2, 2)),
             pltpu.SemaphoreType.DMA((2,)),
             pltpu.SemaphoreType.DMA,
@@ -243,19 +280,21 @@
             pltpu.SemaphoreType.DMA((GATHER_COPIES,)),
         ],
         compiler_params=pltpu.CompilerParams(
-            collective_id=0, has_side_effects=True, vmem_limit_bytes=48 << 20
+            collective_id=0, has_side_effects=True, vmem_limit_bytes=60 << 20
         ),
         name="gather_items",
-    )(items, ratings, observed, spread, bits)
-
-
-def tile_kernel(
-    block_of, tile_user, owner, fetch_block, users, masked, fetched, new_users, partial, slots,
-    user16, user16t,
-):
-    f = pl.program_id(0)
-
-    @pl.when(f == 0)
+    )(items, ratings, observed)
+
+
+GROUP = 8
+
+
+def tile_kernel(tile_user, owner, fetch_block, users, masked, *rest):
+    fetched = rest[:GROUP]
+    new_users, partial, slots, user16, user16t, errors = rest[GROUP:]
+    g = pl.program_id(0)
+
+    @pl.when(g == 0)
     def _():
         def block(b, carry):
             rows = pl.ds(b * BS, BS)
@@ -273,27 +312,36 @@
 
         lax.fori_loop(0, 128, clear, 0)
 
-        def note(g, carry):
-            slots[owner[g]] = g * 2 + fetch_block[g]
+        def note(f, carry):
+            slots[owner[f]] = f * 2 + fetch_block[f]
             return carry
 
         lax.fori_loop(0, FETCHES, note, 0)
 
-    item = fetched[0]
-    total = jnp.zeros((R, BS), jnp.float32)
-    for t in range(2):
-        b = tile_user[f * 2 + t]
-        predicted = lax.dot_general(
-            user16[b], item, (((1,), (1,)), ((), ())), preferred_element_type=jnp.float32
-        )
-        miss = predicted - masked[0, t].astype(jnp.float32)
-        error = jnp.where(miss > -0.5 * ABSENT, miss, 0.0).astype(jnp.bfloat16)
-        total += jnp.dot(user16t[b], error, preferred_element_type=jnp.float32)
-        rows = pl.ds(pl.multiple_of(b * BS, BS), BS)
-        new_users[rows, :] += jnp.dot(error, item, preferred_element_type=jnp.float32)
-    partial[0] = total.astype(jnp.bfloat16)
-
-    @pl.when(f == FETCHES - 1)
+    which = [[tile_user[t, g * GROUP + k] for t in range(2)] for k in range(GROUP)]
+    for k in range(GROUP):
+        for t in range(2):
+            predicted = lax.dot_general(
+                user16[which[k][t]], fetched[k][0], (((1,), (1,)), ((), ())),
+                preferred_element_type=jnp.float32,
+            )
+            miss = predicted - masked[k, t].astype(jnp.float32)
+            errors[k, t] = jnp.where(miss > -0.5 * ABSENT, miss, 0.0).astype(jnp.bfloat16)
+    for k in range(GROUP):
+        total = jnp.zeros((R, BS), jnp.float32)
+        for t in range(2):
+            total += jnp.dot(
+                user16t[which[k][t]], errors[k, t], preferred_element_type=jnp.float32
+            )
+        partial[k] = total.astype(jnp.bfloat16)
+    for k in range(GROUP):
+        for t in range(2):
+            rows = pl.ds(pl.multiple_of(which[k][t] * BS, BS), BS)
+            new_users[rows, :] += jnp.dot(
+                errors[k, t], fetched[k][0], preferred_element_type=jnp.float32
+            )
+
+    @pl.when(g == pl.num_programs(0) - 1)
     def _():
         def block(b, carry):
             rows = pl.ds(b * BS, BS)
@@ -303,25 +351,39 @@
         lax.fori_loop(0, 8, block, 0)
 
 
-def tiles(block_of, tile_user, owner, fetch_block, users, masked, fetched):
+def tiles(tile_user, owner, fetch_block, users, masked, fetched):
+    def item(k):
+        def place(g, tile_user, owner, fetch_block):
+            f = g * GROUP + k
+            chip, mine = owner[f] // 2, lax.axis_index("rows") // 2
+            away = (
+                lax.rem(chip // 16 + 4 - mine // 16, 4) * 16
+                + lax.rem(lax.rem(chip // 4, 4) + 4 - lax.rem(mine // 4, 4), 4) * 4
+                + lax.rem(lax.rem(chip, 4) + 4 - lax.rem(mine, 4), 4)
+            )
+            return (lax.rem(owner[f], 2) * 64 + away) * 2 + fetch_block[f], 0, 0
+
+        return pl.BlockSpec((1, BS, R), place)
+
     return pl.pallas_call(
         tile_kernel,
         grid_spec=pltpu.PrefetchScalarGridSpec(
-            num_scalar_prefetch=4,
-            grid=(FETCHES,),
+            num_scalar_prefetch=3,
+            grid=(FETCHES // GROUP,),
             in_specs=[
-                pl.BlockSpec(users.shape, lambda f, *_: (0, 0)),
-                pl.BlockSpec((1, 2, BS, BS), lambda f, *_: (f, 0, 0, 0)),
-                pl.BlockSpec((1, BS, R), lambda f, block_of, *_: (block_of[f], 0, 0)),
+                pl.BlockSpec(users.shape, lambda g, *_: (0, 0)),
+                pl.BlockSpec((GROUP, 2, BS, BS), lambda g, *_: (g, 0, 0, 0)),
+                *[item(k) for k in range(GROUP)],
             ],
             out_specs=[
-                pl.BlockSpec(users.shape, lambda f, *_: (0, 0)),
-                pl.BlockSpec((1, R, BS), lambda f, *_: (f, 0, 0)),
+                pl.BlockSpec(users.shape, lambda g, *_: (0, 0)),
+                pl.BlockSpec((GROUP, R, BS), lambda g, *_: (g, 0, 0)),
                 pl.BlockSpec(memory_space=pltpu.SMEM),
             ],
             scratch_shapes=[
                 pltpu.VMEM((8, BS, R), jnp.bfloat16),
                 pltpu.VMEM((8, R, BS), jnp.bfloat16),
+                pltpu.VMEM((GROUP, 2, BS, BS), jnp.bfloat16),
             ],
         ),
         out_shape=(
@@ -331,17 +393,17 @@
         ),
         compiler_params=pltpu.CompilerParams(vmem_limit_bytes=48 << 20),
         name="tile_gradients",
-    )(block_of, tile_user, owner, fetch_block, users, masked, fetched)
+    )(tile_user, owner, fetch_block, users, masked, *([fetched] * GROUP))
 
 
 REDUCE_COPIES = 48 + 3 * (4 + 4 + 4 + 3 + 3)
 
 
 def reduce_kernel(
-    slots, partial, items, new_items,
-    parts, outgoing0, outgoing1, outgoing2, arriving0, arriving1, arriving2, dense0, dense1, dense2,
+    slots, parts, item_grad,
+    outgoing0, outgoing1, outgoing2, arriving0, arriving1, arriving2, dense0, dense1, dense2,
     far0, far1, far2, near0, near1, near2, plane0, plane1, plane2, line0, line1, line2,
-    row0, row1, row2, unit0, unit1, unit2, grad, load_sem, send_sems, recv_sems,
+    row0, row1, row2, unit0, unit1, unit2, grad, send_sems, recv_sems,
 ):
     outgoing, arriving = (outgoing0, outgoing1, outgoing2), (arriving0, arriving1, arriving2)
     dense, far, near = (dense0, dense1, dense2), (far0, far1, far2), (near0, near1, near2)
@@ -350,11 +412,8 @@
     where = position()
     core = where[3]
     twin = sibling(where)
-    load = pltpu.make_async_copy(partial, parts, load_sem)
-    load.start()
     net = Sender(send_sems, recv_sems)
     greet(where)
-    load.wait()
     thirds = range(3)
 
     def fill(target, p, parity, d3, d2):
@@ -483,25 +542,23 @@
         grad[pl.ds(start, count), :] = total
     for block in range(2):
         rows = pl.ds(block * BS, BS)
-        new_items[rows, :] = items[rows, :] - LEARN_RATE * grad[pl.ds(block * R, R), :].T
+        item_grad[rows, :] = grad[pl.ds(block * R, R), :].T
     net.finish()
 
 
-def reduce_items(slots, partial, items):
+def reduce_items(slots, partial):
     def each(*lead):
         return [pltpu.VMEM((*lead, count, BS), jnp.bfloat16) for _, count in REDUCE_ROWS]
 
     return pl.pallas_call(
         reduce_kernel,
-        out_shape=jax.ShapeDtypeStruct(items.shape, jnp.float32),
+        out_shape=jax.ShapeDtypeStruct((2 * BS, R), jnp.float32),
         in_specs=[
             pl.BlockSpec(memory_space=pltpu.SMEM),
-            pl.BlockSpec(memory_space=pl.ANY),
             pl.BlockSpec(memory_space=pltpu.VMEM),
         ],
         out_specs=pl.BlockSpec(memory_space=pltpu.VMEM),
         scratch_shapes=[
-            pltpu.VMEM(partial.shape, jnp.bfloat16),
             *each(4, 4, 4),
             *each(4, 4, 4),
             *each(4, 4, 4),
@@ -512,38 +569,25 @@
             *each(4),
             *each(3),
             pltpu.VMEM((BS, BS), jnp.float32),
-            pltpu.SemaphoreType.DMA,
             pltpu.SemaphoreType.DMA((REDUCE_COPIES,)),
             pltpu.SemaphoreType.DMA((REDUCE_COPIES,)),
         ],
         compiler_params=pltpu.CompilerParams(
-            collective_id=1, has_side_effects=True, vmem_limit_bytes=56 << 20
+            collective_id=1, has_side_effects=True, vmem_limit_bytes=44 << 20
         ),
         name="reduce_items",
-    )(slots, partial, items)
+    )(slots, partial)
 
 
 def body(users, items, ratings, observed, tile_user, fetch_owner, fetch_block):
     owner = fetch_owner[:, 0]
-    chip = owner // 2
-    mine = lax.axis_index("rows") // 2
-    away = (
-        (chip // 16 - mine // 16) % 4 * 16
-        + (chip // 4 % 4 - mine // 4 % 4) % 4 * 4
-        + (chip % 4 - mine % 4) % 4
-    )
-    block_of = ((owner % 2) * 64 + away) * 2 + fetch_block
-    word = jnp.arange(128, dtype=jnp.int32)[:, None]
-    column = jnp.arange(BS, dtype=jnp.int32)[None, :]
-    spread = (word % 32 == column // 8).astype(jnp.bfloat16)
-    bits = jnp.broadcast_to(jnp.left_shift(1, column % 8), (BS, BS))
     packed = observed.reshape(FETCHES, 2, 64, 128).transpose(0, 2, 1, 3).reshape(FETCHES, 128, 128)
-    gathered, masked = gather(items, ratings, packed, spread, bits)
+    gathered, masked = gather(items, ratings, packed)
     new_users, partial, slots = tiles(
-        block_of, tile_user.reshape(-1), owner, fetch_block, users, masked,
+        tile_user.T, owner, fetch_block, users, masked,
         gathered.reshape(256, BS, R),
     )
-    new_items = reduce_items(slots, partial, items)
+    new_items = items - LEARN_RATE * reduce_items(slots, partial)
     return (new_users, new_items)
 
 

time: 183 us -> 127 us (0.69); the launches traced: 181 us -> 127 us
  Pallas kernels: 171 us -> 125 us
  local copies, waits for them, and re-layouts: 8.18 us -> 0.02 us
    pallas_call x1, Pallas kernels: 56.1 us -> 26.4 us  [tiles(): pl.pallas_call(tile_kernel, grid_spec=pltpu.PrefetchScalarGridSpec(num_sc...]
    pallas_call x1, Pallas kernels: 65.7 us -> 50.1 us  [gather(): pl.pallas_call(gather_kernel, out_shape=(jax.ShapeDtypeStruct((2, 4, 4, 4...]
    unnamed x16 -> x10, local copies, waits for them, and re-layouts: 8.02 us -> 0.02 us
where the time goes in v2:
time: 127 us
  Pallas kernels  125 us (98%)
    pallas_call x1, Pallas kernels, gather(): pl.pallas_call(gather_kernel, out_shape=(jax.ShapeDtypeStruct((2, 4, 4, 4...  50.1 us
    pallas_call x1, Pallas kernels, reduce_items(): pl.pallas_call(reduce_kernel, out_shape=jax.ShapeDtypeStruct((2 * BS, R),...  48.6 us
    pallas_call x1, Pallas kernels, tiles(): pl.pallas_call(tile_kernel, grid_spec=pltpu.PrefetchScalarGridSpec(num_sc...  26.4 us

profile of v2, /device:TPU:0, one launch (start us, length us, event | category | flops | bytes accessed | tf_op | source)
XLA Modules:
  0.0 126.6 jit_solution(2523444494678724282)
XLA Ops:
  0.6 0.0 copy-start.3
  0.6 0.0 copy-start.2
  0.7 0.0 copy-start.1
  0.7 0.0 copy-start
  0.7 50.1 %gather_items.1 = (bf16[2,4,4,4,512,128]{5,4,3,2,1,0:T(8,128)(2,1)}, bf16[64,2,256,256]{3,2,1,0:T(8,128)(2,1)}) custom-call(f32[512,128]{1,0:T(8,128)} %items.1, bf16[64,2,256,256]{3,2,1,0:T(8,128)(2,1)} %ratings.1, s32[64,128,128]{2,1,0:T(8,128)} %bitcast.18), custom_call_target="tpu_custom_call" | custom-call | tf_op jit(solution)/shard_map/gather_items/pallas_call | solution.py:256
  50.8 0.0 copy-done.3
  50.8 0.0 copy-done.2
  50.8 0.0 copy-done.1
  50.8 0.0 copy-done
  50.8 0.0 copy-start.4
  50.8 26.4 %tile_gradients.1 = (f32[2048,128]{1,0:T(8,128)}, bf16[64,128,256]{2,1,0:T(8,128)(2,1)S(1)}, s32[128]{0:T(128)S(1)}) custom-call(s32[2,64]{1,0:T(2,128)S(1)} %bitcast.8, s32[64]{0:T(128)S(1)} %bitcast.9, s32[64]{0:T(128)S(1)} %copy-done.3, f32[2048,128]{1,0:T(8,128)S(1)} %copy-done, bf16[64,2,256,256]{3,2,1,0:T(8,128)(2,1)} %get-tuple-element.7.masked, ...), custom_call_target="tpu_custom_call" | custom-call | tf_op jit(solution)/shard_map/tile_gradients/pallas_call | solution.py:368
  77.2 48.6 %reduce_items.1 = f32[512,128]{1,0:T(8,128)S(1)} custom-call(s32[128]{0:T(128)S(1)} %get-tuple-element.10.slots, bf16[64,128,256]{2,1,0:T(8,128)(2,1)S(1)} %get-tuple-element.11.parts), custom_call_target="tpu_custom_call" | custom-call | tf_op jit(solution)/shard_map/reduce_items/pallas_call | solution.py:553
  125.8 0.0 copy-done.4
  125.8 0.7 multiply_subtract_fusion
Async XLA Ops:
  0.6 50.1 %copy-start.3 = (s32[64]{0:T(128)S(1)}, s32[64]{0:T(128)}, u32[]{:S(2)}) copy-start(s32[64]{0:T(128)} %fetch_block.1) | copy-start | bytes 772
  0.6 50.1 %copy-start.2 = (s32[64,1]{0,1:T(1,128)S(1)}, s32[64,1]{0,1:T(1,128)}, u32[]{:S(2)}) copy-start(s32[64,1]{0,1:T(1,128)} %param.12) | copy-start | bytes 772
  0.7 50.1 %copy-start.1 = (s32[64,2]{0,1:T(2,128)S(1)}, s32[64,2]{0,1:T(2,128)}, u32[]{:S(2)}) copy-start(s32[64,2]{0,1:T(2,128)} %param.11) | copy-start | bytes 1540
  0.7 50.1 %copy-start = (f32[2048,128]{1,0:T(8,128)S(1)}, f32[2048,128]{1,0:T(8,128)}, u32[]{:S(2)}) copy-start(f32[2048,128]{1,0:T(8,128)} %users.1) | copy-start | bytes 3145732
  50.8 75.0 %copy-start.4 = (f32[512,128]{1,0:T(8,128)S(1)}, f32[512,128]{1,0:T(8,128)}, u32[]{:S(2)}) copy-start(f32[512,128]{1,0:T(8,128)} %items.1) | copy-start | bytes 786436

commit v3 on v2

--- a/solution.py
+++ b/solution.py
@@ -9,6 +9,7 @@
 
 LEARN_RATE = 0.02
 MESH = pl.DeviceIdType.MESH
+in_space = pltpu.with_memory_space_constraint
 R = 128
 BS = 256
 FETCHES = 64
@@ -43,7 +44,7 @@
     partners = [shifted(where, a, s) for a in range(3) for s in (1, -1, 2)] + [sibling(where)]
     for partner in partners:
         pl.semaphore_signal(barrier, inc=1, device_id=(partner,), device_id_type=MESH)
-    pl.semaphore_wait(barrier, len(partners))
+    return lambda: pl.semaphore_wait(barrier, len(partners))
 
 
 class Sender:
@@ -69,12 +70,12 @@
             copy.wait_send()
 
 
-GATHER_COPIES = 3 * (3 + 4 + 12 + 6) + 1 + 3 * (5 + 12 + 6)
+GATHER_COPIES = 3 * (3 + 4 + 14 + 7) + 1 + 3 * (6 + 14 + 7)
 
 
 def gather_kernel(
-    items, ratings, observed, gathered, masked,
-    spread, wide_own, own, words, rate_in, obs_in, rate_out, in_sems, out_sems, own_sem, send_sems, recv_sems,
+    items, ratings, observed, users, gathered, masked, user16, user16t,
+    spread, wide_own, own, words, rate_in, obs_in, wide_users, in_sems, own_sem, user_sem, send_sems, recv_sems,
 ):
     where = position()
     core = where[3]
@@ -87,11 +88,6 @@
             pltpu.make_async_copy(observed.at[some], obs_in.at[slot], in_sems.at[1, slot]),
         )
 
-    def fetch_out(n, slot):
-        return pltpu.make_async_copy(
-            rate_out.at[slot], masked.at[pl.ds(n * CHUNK, CHUNK)], out_sems.at[slot]
-        )
-
     def one(n, carry):
         slot = lax.rem(n, 2)
 
@@ -102,10 +98,6 @@
 
         for copy in fetch_in(n, slot):
             copy.wait()
-
-        @pl.when(n >= 2)
-        def _():
-            fetch_out(n - 2, slot).wait()
 
         lane_group = lax.broadcasted_iota(jnp.int32, (64, 128), 1) // 32
         bit = jnp.left_shift(1, lax.broadcasted_iota(jnp.int32, (1, BS), 1) % 8)
@@ -121,13 +113,12 @@
                     words[t].astype(jnp.bfloat16), spread[...], preferred_element_type=jnp.float32
                 )
                 seen = (wide.astype(jnp.int32) & bit) != 0
-                rate_out[slot, k, t] = jnp.where(
+                masked[n * CHUNK + k, t] = jnp.where(
                     seen, rate_in[slot, k, t].astype(jnp.float32), ABSENT
                 ).astype(jnp.bfloat16)
             return carry
 
         lax.fori_loop(0, CHUNK, fetch, 0)
-        fetch_out(n, slot).start()
         return carry
 
     def work(first, last):
@@ -141,18 +132,21 @@
 
     every = slice(None)
     here = gathered.at[core, 0, 0, 0]
-    word = lax.broadcasted_iota(jnp.int32, (128, BS), 0)
-    column = lax.broadcasted_iota(jnp.int32, (128, BS), 1)
-    spread[...] = jnp.where(word % 32 == column // 8, 1.0, 0.0).astype(jnp.bfloat16)
+    greeted = greet(where)
     read = pltpu.make_async_copy(items, wide_own, own_sem)
     read.start()
     for copy in fetch_in(0, 0):
         copy.start()
+    read_users = pltpu.make_async_copy(users, wide_users, user_sem)
+    read_users.start()
+    word = lax.broadcasted_iota(jnp.int32, (128, BS), 0)
+    column = lax.broadcasted_iota(jnp.int32, (128, BS), 1)
+    spread[...] = jnp.where(word % 32 == column // 8, 1.0, 0.0).astype(jnp.bfloat16)
     read.wait()
     own[...] = wide_own[...].astype(jnp.bfloat16)
     place = pltpu.make_async_copy(own, here, own_sem)
     place.start()
-    greet(where)
+    greeted()
 
     first, line, plane, pair = {}, {}, {}, []
     twin = sibling(where)
@@ -172,13 +166,20 @@
         for s in (1, -1):
             plane[p, 0, s] = net.send(mine, part(p, 0, 0, -s % 4), shifted(where, a3, s))
     pair.append(net.send(own, here, twin))
+    def halve(b, carry):
+        value = wide_users[pl.ds(b * BS, BS), :]
+        user16[b] = value.astype(jnp.bfloat16)
+        user16t[b] = value.T.astype(jnp.bfloat16)
+        return carry
+
     place.wait()
     work(0, 1)
     low, high = slice(0, 2), slice(2, 4)
     groups = {
-        0: (0, 0), 1: (slice(1, 4), 0), 2: (every, 3), 3: (every, 1), 4: (low, 2), 5: (high, 2)
+        0: (0, 0), 1: (slice(1, 4), 0), 2: (every, 3), 3: (low, 1), 6: (high, 1),
+        4: (low, 2), 5: (high, 2),
     }
-    onward = {0: 1, 1: 1, 2: -1, 3: -1, 4: 1, 5: 1}
+    onward = {0: 1, 1: 1, 2: -1, 3: -1, 6: -1, 4: 1, 5: 1}
 
     def spread_group(p, g):
         a3 = ORDERS[p][2]
@@ -215,6 +216,8 @@
         spread_group(p, 1)
     work(1, 2)
     pass_on(0)
+    read_users.wait()
+    lax.fori_loop(0, 8, halve, 0)
     work(2, 3)
     for g, s, half in ((2, 1, low), (3, -1, high)):
         for p in thirds:
@@ -223,6 +226,8 @@
                 part(p, half, -s % 4, 0), part(p, half, 2, 0), shifted(where, ORDERS[p][1], s)
             )
             spread_group(p, g)
+            if g == 3:
+                spread_group(p, 6)
     work(3, 5)
     pass_on(1)
     work(5, 7)
@@ -235,6 +240,7 @@
     passed(0)
     work(9, 11)
     pass_on(3)
+    pass_on(6)
     passed(1)
     work(11, 13)
     pass_on(4)
@@ -242,29 +248,27 @@
     pass_on(5)
     work(14, STEPS)
     passed(2)
+    passed(4)
     passed(3)
-    for slot in range(2):
-        fetch_out(STEPS - 2 + slot, slot).wait()
-    passed(4)
     passed(5)
+    passed(6)
     for copy in pair:
         copy.wait_recv()
     net.finish()
 
 
-def gather(items, ratings, observed):
+def gather(items, ratings, observed, users):
     return pl.pallas_call(
         gather_kernel,
         out_shape=(
-            jax.ShapeDtypeStruct((2, 4, 4, 4, 512, R), jnp.bfloat16),
-            jax.ShapeDtypeStruct(ratings.shape, jnp.bfloat16),
+            pltpu.HBM((2, 4, 4, 4, 512, R), jnp.bfloat16),
+            pltpu.VMEM(ratings.shape, jnp.bfloat16),
+            pltpu.VMEM((8, BS, R), jnp.bfloat16),
+            pltpu.VMEM((8, R, BS), jnp.bfloat16),
         ),
-        in_specs=[
-            pl.BlockSpec(memory_space=pltpu.HBM),
-            pl.BlockSpec(memory_space=pltpu.HBM),
-            pl.BlockSpec(memory_space=pltpu.HBM),
-        ],
-        out_specs=[pl.BlockSpec(memory_space=pltpu.HBM)] * 2,
+        in_specs=[pl.BlockSpec(memory_space=pltpu.HBM)] * 4,
+        out_specs=[pl.BlockSpec(memory_space=pltpu.HBM)]
+        + [pl.BlockSpec(memory_space=pltpu.VMEM)] * 3,
         scratch_shapes=[
             pltpu.VMEM((128, BS), jnp.bfloat16),
             pltpu.VMEM((512, R), jnp.float32),
@@ -272,131 +276,131 @@
             pltpu.VMEM((2, BS, 128), jnp.float32),
             pltpu.VMEM((2, CHUNK, 2, BS, BS), jnp.bfloat16),
             pltpu.VMEM((2, CHUNK, 128, 128), jnp.int32),
-            pltpu.VMEM((2, CHUNK, 2, BS, BS), jnp.bfloat16),
+            pltpu.VMEM(users.shape, jnp.float32),
             pltpu.SemaphoreType.DMA((2, 2)),
-            pltpu.SemaphoreType.DMA((2,)),
+            pltpu.SemaphoreType.DMA,
             pltpu.SemaphoreType.DMA,
             pltpu.SemaphoreType.DMA((GATHER_COPIES,)),
             pltpu.SemaphoreType.DMA((GATHER_COPIES,)),
         ],
         compiler_params=pltpu.CompilerParams(
-            collective_id=0, has_side_effects=True, vmem_limit_bytes=60 << 20
+            collective_id=0, has_side_effects=True, vmem_limit_bytes=12 << 20
         ),
         name="gather_items",
-    )(items, ratings, observed)
+    )(*[in_space(x, pltpu.HBM) for x in (items, ratings, observed, users)])
 
 
 GROUP = 8
-
-
-def tile_kernel(tile_user, owner, fetch_block, users, masked, *rest):
-    fetched = rest[:GROUP]
-    new_users, partial, slots, user16, user16t, errors = rest[GROUP:]
-    g = pl.program_id(0)
-
-    @pl.when(g == 0)
-    def _():
-        def block(b, carry):
-            rows = pl.ds(b * BS, BS)
-            value = users[rows, :]
-            user16[b] = value.astype(jnp.bfloat16)
-            user16t[b] = value.T.astype(jnp.bfloat16)
-            new_users[rows, :] = jnp.zeros((BS, R), jnp.float32)
-            return carry
-
-        lax.fori_loop(0, 8, block, 0)
-
-        def clear(o, carry):
-            slots[o] = -1
-            return carry
-
-        lax.fori_loop(0, 128, clear, 0)
-
-        def note(f, carry):
-            slots[owner[f]] = f * 2 + fetch_block[f]
-            return carry
-
-        lax.fori_loop(0, FETCHES, note, 0)
-
-    which = [[tile_user[t, g * GROUP + k] for t in range(2)] for k in range(GROUP)]
-    for k in range(GROUP):
-        for t in range(2):
-            predicted = lax.dot_general(
-                user16[which[k][t]], fetched[k][0], (((1,), (1,)), ((), ())),
-                preferred_element_type=jnp.float32,
-            )
-            miss = predicted - masked[k, t].astype(jnp.float32)
-            errors[k, t] = jnp.where(miss > -0.5 * ABSENT, miss, 0.0).astype(jnp.bfloat16)
-    for k in range(GROUP):
-        total = jnp.zeros((R, BS), jnp.float32)
-        for t in range(2):
-            total += jnp.dot(
-                user16t[which[k][t]], errors[k, t], preferred_element_type=jnp.float32
-            )
-        partial[k] = total.astype(jnp.bfloat16)
-    for k in range(GROUP):
-        for t in range(2):
-            rows = pl.ds(pl.multiple_of(which[k][t] * BS, BS), BS)
-            new_users[rows, :] += jnp.dot(
-                errors[k, t], fetched[k][0], preferred_element_type=jnp.float32
-            )
-
-    @pl.when(g == pl.num_programs(0) - 1)
-    def _():
-        def block(b, carry):
-            rows = pl.ds(b * BS, BS)
-            new_users[rows, :] = users[rows, :] - LEARN_RATE * new_users[rows, :]
-            return carry
-
-        lax.fori_loop(0, 8, block, 0)
-
-
-def tiles(tile_user, owner, fetch_block, users, masked, fetched):
-    def item(k):
-        def place(g, tile_user, owner, fetch_block):
-            f = g * GROUP + k
-            chip, mine = owner[f] // 2, lax.axis_index("rows") // 2
-            away = (
-                lax.rem(chip // 16 + 4 - mine // 16, 4) * 16
-                + lax.rem(lax.rem(chip // 4, 4) + 4 - lax.rem(mine // 4, 4), 4) * 4
-                + lax.rem(lax.rem(chip, 4) + 4 - lax.rem(mine, 4), 4)
-            )
-            return (lax.rem(owner[f], 2) * 64 + away) * 2 + fetch_block[f], 0, 0
-
-        return pl.BlockSpec((1, BS, R), place)
-
+GROUPS = FETCHES // GROUP
+
+
+def tile_kernel(
+    tile_user, owner, fetch_block, users, user16, user16t, masked, fetched,
+    new_users, partial, slots, blocks, errors, grad, in_sems, out_sems,
+):
+    where = position()
+
+    def read(f):
+        chip = owner[f] // 2
+        at = (chip // 16, lax.rem(chip // 4, 4), lax.rem(chip, 4))
+        dy, dz, dx = [lax.rem(a + 4 - w, 4) for a, w in zip(at, where)]
+        away = ((lax.rem(owner[f], 2) * 4 + dy) * 4 + dz) * 4 + dx
+        return pltpu.make_async_copy(
+            fetched.at[away * 2 + fetch_block[f]], blocks.at[f], in_sems.at[f]
+        )
+
+    def write(b):
+        rows = pl.ds(b * BS, BS)
+        return pltpu.make_async_copy(grad.at[rows], new_users.at[rows], out_sems.at[b])
+
+    for f in range(2 * GROUP):
+        read(f).start()
+    grad[...] = jnp.zeros_like(grad)
+
+    def one(g, carry):
+        @pl.when(g + 2 < GROUPS)
+        def _():
+            for k in range(GROUP):
+                read((g + 2) * GROUP + k).start()
+
+        @pl.when(g < GROUPS // 2)
+        def _():
+            for k in range(32):
+                slots[g * 32 + k] = -1
+
+        @pl.when(g >= GROUPS // 2)
+        def _():
+            for k in range(16):
+                f = (g - GROUPS // 2) * 16 + k
+                slots[owner[f]] = f * 2 + fetch_block[f]
+
+        fetches = [g * GROUP + k for k in range(GROUP)]
+        which = [[tile_user[t, f] for t in range(2)] for f in fetches]
+        for f in fetches:
+            pltpu.make_async_copy(fetched.at[0], blocks.at[f], in_sems.at[f]).wait()
+        for k, f in enumerate(fetches):
+            for t in range(2):
+                predicted = lax.dot_general(
+                    user16[which[k][t]], blocks[f], (((1,), (1,)), ((), ())),
+                    preferred_element_type=jnp.float32,
+                )
+                miss = predicted - masked[f, t].astype(jnp.float32)
+                errors[k, t] = jnp.where(miss > -0.5 * ABSENT, miss, 0.0).astype(jnp.bfloat16)
+        for k, f in enumerate(fetches):
+            total = jnp.zeros((R, BS), jnp.float32)
+            for t in range(2):
+                total += jnp.dot(
+                    user16t[which[k][t]], errors[k, t], preferred_element_type=jnp.float32
+                )
+            partial[f] = total.astype(jnp.bfloat16)
+        for k, f in enumerate(fetches):
+            for t in range(2):
+                rows = pl.ds(pl.multiple_of(which[k][t] * BS, BS), BS)
+                grad[rows, :] += jnp.dot(
+                    errors[k, t], blocks[f], preferred_element_type=jnp.float32
+                )
+        return carry
+
+    lax.fori_loop(0, GROUPS, one, 0)
+
+    def step(b, carry):
+        rows = pl.ds(b * BS, BS)
+        grad[rows, :] = users[rows, :] - LEARN_RATE * grad[rows, :]
+        write(b).start()
+        return carry
+
+    lax.fori_loop(0, 8, step, 0)
+    for b in range(8):
+        write(b).wait()
+
+
+def tiles(tile_user, owner, fetch_block, users, user16, user16t, masked, fetched):
+    smem, vmem, hbm = [
+        pl.BlockSpec(memory_space=m) for m in (pltpu.SMEM, pltpu.VMEM, pltpu.HBM)
+    ]
+    held = [in_space(x, pltpu.VMEM) for x in (users, user16, user16t, masked)]
     return pl.pallas_call(
         tile_kernel,
-        grid_spec=pltpu.PrefetchScalarGridSpec(
-            num_scalar_prefetch=3,
-            grid=(FETCHES // GROUP,),
-            in_specs=[
-                pl.BlockSpec(users.shape, lambda g, *_: (0, 0)),
-                pl.BlockSpec((GROUP, 2, BS, BS), lambda g, *_: (g, 0, 0, 0)),
-                *[item(k) for k in range(GROUP)],
-            ],
-            out_specs=[
-                pl.BlockSpec(users.shape, lambda g, *_: (0, 0)),
-                pl.BlockSpec((GROUP, R, BS), lambda g, *_: (g, 0, 0)),
-                pl.BlockSpec(memory_space=pltpu.SMEM),
-            ],
-            scratch_shapes=[
-                pltpu.VMEM((8, BS, R), jnp.bfloat16),
-                pltpu.VMEM((8, R, BS), jnp.bfloat16),
-                pltpu.VMEM((GROUP, 2, BS, BS), jnp.bfloat16),
-            ],
-        ),
         out_shape=(
-            jax.ShapeDtypeStruct(users.shape, jnp.float32),
-            jax.ShapeDtypeStruct((FETCHES, R, BS), jnp.bfloat16),
+            pltpu.HBM(users.shape, jnp.float32),
+            pltpu.VMEM((FETCHES, R, BS), jnp.bfloat16),
             jax.ShapeDtypeStruct((128,), jnp.int32),
         ),
-        compiler_params=pltpu.CompilerParams(vmem_limit_bytes=48 << 20),
+        in_specs=[smem, smem, smem, vmem, vmem, vmem, vmem, hbm],
+        out_specs=[hbm, vmem, smem],
+        scratch_shapes=[
+            pltpu.VMEM((FETCHES, BS, R), jnp.bfloat16),
+            pltpu.VMEM((GROUP, 2, BS, BS), jnp.bfloat16),
+            pltpu.VMEM(users.shape, jnp.float32),
+            pltpu.SemaphoreType.DMA((FETCHES,)),
+            pltpu.SemaphoreType.DMA((8,)),
+        ],
+        compiler_params=pltpu.CompilerParams(vmem_limit_bytes=14 << 20),
         name="tile_gradients",
-    )(tile_user, owner, fetch_block, users, masked, *([fetched] * GROUP))
-
-
-REDUCE_COPIES = 48 + 3 * (4 + 4 + 4 + 3 + 3)
+    )(tile_user, owner, fetch_block, *held, in_space(fetched, pltpu.HBM))
+
+
+REDUCE_COPIES = 48 + 3 * (4 + 4 + 4 + 6 + 3)
 
 
 def reduce_kernel(
@@ -413,7 +417,7 @@
     core = where[3]
     twin = sibling(where)
     net = Sender(send_sems, recv_sems)
-    greet(where)
+    greeted = greet(where)
     thirds = range(3)
 
     def fill(target, p, parity, d3, d2):
@@ -441,9 +445,12 @@
 
     pair = {}
 
+    def prepare(d3, d2):
+        for p in thirds:
+            fill(outgoing[p], p, 1 - core, d3, d2)
+
     def hand_over(d3, d2):
         for p in thirds:
-            fill(outgoing[p], p, 1 - core, d3, d2)
             pair[p, d3, d2] = net.send(
                 outgoing[p].at[d3, d2], arriving[p].at[d3, d2], twin
             )
@@ -454,14 +461,17 @@
             pair[p, d3, d2].wait_recv()
             add_into(dense[p].at[d3, d2], arriving[p].at[d3, d2])
 
-    def add_into(target, other):
+    def add_into(target, other, count=4):
         def one(n, carry):
             target[n] = (target[n].astype(jnp.float32) + other[n].astype(jnp.float32)).astype(
                 jnp.bfloat16
             )
             return carry
 
-        lax.fori_loop(0, 4, one, 0)
+        lax.fori_loop(0, count, one, 0)
+
+    def add_two(target, other):
+        add_into(target, other, 2)
 
     via = {0: 1, 1: 1, 2: -1, 3: -1}
     relay, direct = {}, {}
@@ -486,7 +496,10 @@
 
     todo = [(2, 0), (2, 2), (2, 1), (2, 3), (1, 2), (3, 0), (1, 3), (3, 1)]
     todo += [(1, 0), (3, 2), (1, 1), (3, 3), (0, 0), (0, 1), (0, 2), (0, 3)]
-    ahead = 4
+    ahead = 2
+    for d3, d2 in todo[:ahead]:
+        prepare(d3, d2)
+    greeted()
     for d3, d2 in todo[:ahead]:
         hand_over(d3, d2)
     for n, (d3, d2) in enumerate(todo):
@@ -496,7 +509,13 @@
         elif d3 != 0:
             send_near(d2, 1 if d3 == 1 else -1)
         if n + ahead < len(todo):
+            prepare(*todo[n + ahead])
             hand_over(*todo[n + ahead])
+
+    low, high = pl.ds(0, 2), pl.ds(2, 2)
+
+    def to_line(p, name, src, dst, s):
+        direct[p, name] = net.send(src, dst, shifted(where, ORDERS[p][1], s))
 
     for d2 in (2, 1, 3, 0):
         for p in thirds:
@@ -511,18 +530,27 @@
                 return carry
 
             lax.fori_loop(0, 4, one, 0)
-            if d2 != 0:
-                s = {1: 1, 2: 2, 3: -1}[d2]
-                direct[p, "line", s] = net.send(
-                    plane[p].at[d2], line[p].at[d2 - 1], shifted(where, ORDERS[p][1], s)
-                )
+            if d2 == 2:
+                to_line(p, "far+", plane[p].at[2, low], line[p].at[2, low], 1)
+                to_line(p, "far-", plane[p].at[2, high], line[p].at[2, high], -1)
+            elif d2 == 1:
+                to_line(p, "near+", plane[p].at[1, high], line[p].at[0, high], 1)
+            elif d2 == 3:
+                to_line(p, "near-", plane[p].at[3, low], line[p].at[1, low], -1)
     for p in thirds:
-        for s in (1, -1, 2):
-            direct[p, "line", s].wait_recv()
+        direct[p, "far+"].wait_recv()
+        add_two(plane[p].at[1, low], line[p].at[2, low])
+        to_line(p, "last+", plane[p].at[1, low], line[p].at[0, low], 1)
+        direct[p, "far-"].wait_recv()
+        add_two(plane[p].at[3, high], line[p].at[2, high])
+        to_line(p, "last-", plane[p].at[3, high], line[p].at[1, high], -1)
+    for p in thirds:
+        for name in ("near+", "near-", "last+", "last-"):
+            direct[p, name].wait_recv()
 
         def one(n, carry, p=p):
             total = plane[p][0, n].astype(jnp.float32)
-            for k in range(3):
+            for k in range(2):
                 total += line[p][k, n].astype(jnp.float32)
             row[p][n] = total.astype(jnp.bfloat16)
             return carry
@@ -573,18 +601,18 @@
             pltpu.SemaphoreType.DMA((REDUCE_COPIES,)),
         ],
         compiler_params=pltpu.CompilerParams(
-            collective_id=1, has_side_effects=True, vmem_limit_bytes=44 << 20
+            collective_id=1, has_side_effects=True, vmem_limit_bytes=38 << 20
         ),
         name="reduce_items",
-    )(slots, partial)
+    )(slots, in_space(partial, pltpu.VMEM))
 
 
 def body(users, items, ratings, observed, tile_user, fetch_owner, fetch_block):
     owner = fetch_owner[:, 0]
     packed = observed.reshape(FETCHES, 2, 64, 128).transpose(0, 2, 1, 3).reshape(FETCHES, 128, 128)
-    gathered, masked = gather(items, ratings, packed)
+    gathered, masked, user16, user16t = gather(items, ratings, packed, users)
     new_users, partial, slots = tiles(
-        tile_user.T, owner, fetch_block, users, masked,
+        tile_user.T, owner, fetch_block, users, user16, user16t, masked,
         gathered.reshape(256, BS, R),
     )
     new_items = items - LEARN_RATE * reduce_items(slots, partial)

time: 127 us -> 116 us (0.913)
  Pallas kernels: 125 us -> 114 us
    pallas_call x2, Pallas kernels: 76.5 us -> 67.6 us  [the longest x1 48.6 us: gather(): pl.pallas_call(gather_kernel, out_shape=(pltpu.HBM((2, 4, 4, 4, 512, R),...]
    pallas_call x1, Pallas kernels: 48.6 us -> 46.5 us  [reduce_items(): pl.pallas_call(reduce_kernel, out_shape=jax.ShapeDtypeStruct((2 * BS, R),...]
where the time goes in v3:
time: 116 us
  Pallas kernels  114 us (98%)
    pallas_call x1, Pallas kernels, gather(): pl.pallas_call(gather_kernel, out_shape=(pltpu.HBM((2, 4, 4, 4, 512, R),...  48.6 us
    pallas_call x1, Pallas kernels, reduce_items(): pl.pallas_call(reduce_kernel, out_shape=jax.ShapeDtypeStruct((2 * BS, R),...  46.5 us
    pallas_call x1, Pallas kernels, tiles(): pl.pallas_call(tile_kernel, out_shape=(pltpu.HBM(users.shape, jnp.float32...  19 us

profile of v3, /device:TPU:0, one launch (start us, length us, event | category | flops | bytes accessed | tf_op | source)
XLA Modules:
  0.0 115.6 jit_solution(5159104983621260134)
XLA Ops:
  0.6 0.0 copy-start
  0.6 0.0 copy-start.3
  0.7 0.0 copy-start.2
  0.7 0.0 copy-start.1
  0.7 48.6 %gather_items.1 = (bf16[2,4,4,4,512,128]{5,4,3,2,1,0:T(8,128)(2,1)}, bf16[64,2,256,256]{3,2,1,0:T(8,128)(2,1)S(1)}, bf16[8,256,128]{2,1,0:T(8,128)(2,1)S(1)}, bf16[8,128,256]{2,1,0:T(8,128)(2,1)S(1)}) custom-call(f32[512,128]{1,0:T(8,128)} %items.1, bf16[64,2,256,256]{3,2,1,0:T(8,128)(2,1)} %ratings.1, s32[64,128,128]{2,1,0:T(8,128)} %bitcast.11, ...), custom_call_target="tpu_custom_call" | custom-call | tf_op jit(solution)/shard_map/gather_items/pallas_call | solution.py:261
  49.2 0.0 copy-done
  49.2 0.0 copy-done.3
  49.3 0.0 copy-done.2
  49.3 0.0 copy-done.1
  49.3 0.0 copy-start.4
  49.3 19.0 %tile_gradients.1 = (f32[2048,128]{1,0:T(8,128)}, bf16[64,128,256]{2,1,0:T(8,128)(2,1)S(1)}, s32[128]{0:T(128)S(1)}) custom-call(s32[2,64]{1,0:T(2,128)S(1)} %bitcast.8, s32[64]{0:T(128)S(1)} %bitcast.9, s32[64]{0:T(128)S(1)} %copy-done.3, f32[2048,128]{1,0:T(8,128)S(1)} %copy-done, bf16[8,256,128]{2,1,0:T(8,128)(2,1)S(1)} %get-tuple-element.9.user16, ...), custom_call_target="tpu_custom_call" | custom-call | tf_op jit(solution)/shard_map/tile_gradients/pallas_call | solution.py:382
  68.3 46.5 %reduce_items.1 = f32[512,128]{1,0:T(8,128)S(1)} custom-call(s32[128]{0:T(128)S(1)} %get-tuple-element.14.slots, bf16[64,128,256]{2,1,0:T(8,128)(2,1)S(1)} %get-tuple-element.15.parts), custom_call_target="tpu_custom_call" | custom-call | tf_op jit(solution)/shard_map/reduce_items/pallas_call | solution.py:581
  114.8 0.0 copy-done.4
  114.8 0.8 multiply_subtract_fusion
Async XLA Ops:
  0.6 48.6 %copy-start = (f32[2048,128]{1,0:T(8,128)S(1)}, f32[2048,128]{1,0:T(8,128)}, u32[]{:S(2)}) copy-start(f32[2048,128]{1,0:T(8,128)} %users.3) | copy-start | bytes 3145732
  0.6 48.6 %copy-start.3 = (s32[64]{0:T(128)S(1)}, s32[64]{0:T(128)}, u32[]{:S(2)}) copy-start(s32[64]{0:T(128)} %fetch_block.1) | copy-start | bytes 772
  0.7 48.6 %copy-start.2 = (s32[64,1]{0,1:T(1,128)S(1)}, s32[64,1]{0,1:T(1,128)}, u32[]{:S(2)}) copy-start(s32[64,1]{0,1:T(1,128)} %param.12) | copy-start | bytes 772
  0.7 48.6 %copy-start.1 = (s32[64,2]{0,1:T(2,128)S(1)}, s32[64,2]{0,1:T(2,128)}, u32[]{:S(2)}) copy-start(s32[64,2]{0,1:T(2,128)} %param.11) | copy-start | bytes 1540
  49.3 65.5 %copy-start.4 = (f32[512,128]{1,0:T(8,128)S(1)}, f32[512,128]{1,0:T(8,128)}, u32[]{:S(2)}) copy-start(f32[512,128]{1,0:T(8,128)} %items.1) | copy-start | bytes 786436

commit v4 on v3

--- a/solution.py
+++ b/solution.py
@@ -18,8 +18,7 @@
 ABSENT = 1e30
 
 ORDERS = ((2, 0, 1), (0, 1, 2), (1, 2, 0))
-GATHER_ROWS = ((0, 176), (176, 176), (352, 160))
-REDUCE_ROWS = ((0, 96), (96, 80), (176, 80))
+ROWS = ((0, 176), (176, 176), (352, 160))
 
 
 def position():
@@ -128,17 +127,14 @@
         a1, a2, a3 = ORDERS[p]
         index = [None] * 3
         index[a1], index[a2], index[a3] = d1, d2, d3
-        return gathered.at[(core, *index, pl.ds(*GATHER_ROWS[p]))]
+        return gathered.at[(core, *index, pl.ds(*ROWS[p]))]
 
     every = slice(None)
     here = gathered.at[core, 0, 0, 0]
     greeted = greet(where)
     read = pltpu.make_async_copy(items, wide_own, own_sem)
     read.start()
-    for copy in fetch_in(0, 0):
-        copy.start()
     read_users = pltpu.make_async_copy(users, wide_users, user_sem)
-    read_users.start()
     word = lax.broadcasted_iota(jnp.int32, (128, BS), 0)
     column = lax.broadcasted_iota(jnp.int32, (128, BS), 1)
     spread[...] = jnp.where(word % 32 == column // 8, 1.0, 0.0).astype(jnp.bfloat16)
@@ -146,6 +142,9 @@
     own[...] = wide_own[...].astype(jnp.bfloat16)
     place = pltpu.make_async_copy(own, here, own_sem)
     place.start()
+    for copy in fetch_in(0, 0):
+        copy.start()
+    read_users.start()
     greeted()
 
     first, line, plane, pair = {}, {}, {}, []
@@ -157,12 +156,12 @@
     thirds = range(3)
     for p in thirds:
         a1, a2, a3 = ORDERS[p]
-        mine = own.at[pl.ds(*GATHER_ROWS[p])]
+        mine = own.at[pl.ds(*ROWS[p])]
         for s in (1, -1, 2):
             first[p, s] = net.send(mine, part(p, -s % 4, 0, 0), shifted(where, a1, s))
     for p in thirds:
         a1, a2, a3 = ORDERS[p]
-        mine = own.at[pl.ds(*GATHER_ROWS[p])]
+        mine = own.at[pl.ds(*ROWS[p])]
         for s in (1, -1):
             plane[p, 0, s] = net.send(mine, part(p, 0, 0, -s % 4), shifted(where, a3, s))
     pair.append(net.send(own, here, twin))
@@ -301,10 +300,10 @@
     where = position()
 
     def read(f):
-        chip = owner[f] // 2
-        at = (chip // 16, lax.rem(chip // 4, 4), lax.rem(chip, 4))
-        dy, dz, dx = [lax.rem(a + 4 - w, 4) for a, w in zip(at, where)]
-        away = ((lax.rem(owner[f], 2) * 4 + dy) * 4 + dz) * 4 + dx
+        name = owner[f]
+        at = (name >> 5, name >> 3, name >> 1)
+        dy, dz, dx = [(a - w) & 3 for a, w in zip(at, where)]
+        away = ((name & 1) << 6) + (dy << 4) + (dz << 2) + dx
         return pltpu.make_async_copy(
             fetched.at[away * 2 + fetch_block[f]], blocks.at[f], in_sems.at[f]
         )
@@ -352,7 +351,8 @@
                 total += jnp.dot(
                     user16t[which[k][t]], errors[k, t], preferred_element_type=jnp.float32
                 )
-            partial[f] = total.astype(jnp.bfloat16)
+            partial[f, pl.ds(0, R), :] = total[:, :R].astype(jnp.bfloat16)
+            partial[f, pl.ds(R, R), :] = total[:, R:].astype(jnp.bfloat16)
         for k, f in enumerate(fetches):
             for t in range(2):
                 rows = pl.ds(pl.multiple_of(which[k][t] * BS, BS), BS)
@@ -383,7 +383,7 @@
         tile_kernel,
         out_shape=(
             pltpu.HBM(users.shape, jnp.float32),
-            pltpu.VMEM((FETCHES, R, BS), jnp.bfloat16),
+            pltpu.VMEM((FETCHES, BS, R), jnp.bfloat16),
             jax.ShapeDtypeStruct((128,), jnp.int32),
         ),
         in_specs=[smem, smem, smem, vmem, vmem, vmem, vmem, hbm],
@@ -422,7 +422,7 @@
 
     def fill(target, p, parity, d3, d2):
         a1, a2, a3 = ORDERS[p]
-        start, count = REDUCE_ROWS[p]
+        start, count = ROWS[p]
 
         def one(d1, carry):
             at = [None] * 3
@@ -432,10 +432,10 @@
             code = slots[((at[0] * 4 + at[1]) * 4 + at[2]) * 2 + parity]
             fetch = jnp.maximum(code, 0) // 2
             for block in range(2):
-                low, high = max(start, block * R), min(start + count, (block + 1) * R)
+                low, high = max(start, block * BS), min(start + count, (block + 1) * BS)
                 if low < high:
                     keep = (code >= 0) & (lax.rem(jnp.maximum(code, 0), 2) == block)
-                    value = parts[fetch, pl.ds(low - block * R, high - low), :]
+                    value = parts[fetch, pl.ds(low - block * BS, high - low), :]
                     target[d3, d2, d1, pl.ds(low - start, high - low), :] = jnp.where(
                         keep, value, jnp.zeros_like(value)
                     )
@@ -448,6 +448,8 @@
     def prepare(d3, d2):
         for p in thirds:
             fill(outgoing[p], p, 1 - core, d3, d2)
+        for p in thirds:
+            fill(dense[p], p, core, d3, d2)
 
     def hand_over(d3, d2):
         for p in thirds:
@@ -457,7 +459,6 @@
 
     def collect(d3, d2):
         for p in thirds:
-            fill(dense[p], p, core, d3, d2)
             pair[p, d3, d2].wait_recv()
             add_into(dense[p].at[d3, d2], arriving[p].at[d3, d2])
 
@@ -494,9 +495,9 @@
                 shifted(where, ORDERS[p][2], s),
             )
 
-    todo = [(2, 0), (2, 2), (2, 1), (2, 3), (1, 2), (3, 0), (1, 3), (3, 1)]
-    todo += [(1, 0), (3, 2), (1, 1), (3, 3), (0, 0), (0, 1), (0, 2), (0, 3)]
-    ahead = 2
+    todo = [(2, 0), (2, 2), (2, 1), (2, 3), (1, 2), (3, 1), (1, 3), (3, 2)]
+    todo += [(1, 1), (3, 3), (1, 0), (3, 0), (0, 2), (0, 1), (0, 3), (0, 0)]
+    ahead = 3
     for d3, d2 in todo[:ahead]:
         prepare(d3, d2)
     greeted()
@@ -561,22 +562,22 @@
                 row[p].at[d1], unit[p].at[d1 - 1], shifted(where, ORDERS[p][0], s)
             )
     for p in thirds:
-        start, count = REDUCE_ROWS[p]
+        start, count = ROWS[p]
         for s in (1, -1, 2):
             direct[p, "unit", s].wait_recv()
         total = row[p][0].astype(jnp.float32)
         for k in range(3):
             total += unit[p][k].astype(jnp.float32)
         grad[pl.ds(start, count), :] = total
-    for block in range(2):
-        rows = pl.ds(block * BS, BS)
-        item_grad[rows, :] = grad[pl.ds(block * R, R), :].T
+    for quarter in range(4):
+        rows = pl.ds(quarter * R, R)
+        item_grad[rows, :] = grad[rows, :].T
     net.finish()
 
 
 def reduce_items(slots, partial):
     def each(*lead):
-        return [pltpu.VMEM((*lead, count, BS), jnp.bfloat16) for _, count in REDUCE_ROWS]
+        return [pltpu.VMEM((*lead, count, R), jnp.bfloat16) for _, count in ROWS]
 
     return pl.pallas_call(
         reduce_kernel,
@@ -596,7 +597,7 @@
             *each(3, 4),
             *each(4),
             *each(3),
-            pltpu.VMEM((BS, BS), jnp.float32),
+            pltpu.VMEM((2 * BS, R), jnp.float32),
             pltpu.SemaphoreType.DMA((REDUCE_COPIES,)),
             pltpu.SemaphoreType.DMA((REDUCE_COPIES,)),
         ],

time: 116 us -> 114 us (0.983)
  Pallas kernels: 114 us -> 112 us
where the time goes in v4:
time: 114 us
  Pallas kernels  112 us (98%)
    pallas_call x1, Pallas kernels, gather(): pl.pallas_call(gather_kernel, out_shape=(pltpu.HBM((2, 4, 4, 4, 512, R),...  48.6 us
    pallas_call x1, Pallas kernels, reduce_items(): pl.pallas_call(reduce_kernel, out_shape=jax.ShapeDtypeStruct((2 * BS, R),...  45.5 us
    pallas_call x1, Pallas kernels, tiles(): pl.pallas_call(tile_kernel, out_shape=(pltpu.HBM(users.shape, jnp.float32...  18.3 us

profile of v4, /device:TPU:0, one launch (start us, length us, event | category | flops | bytes accessed | tf_op | source)
XLA Modules:
  0.0 113.9 jit_solution(9583659905675931146)
XLA Ops:
  0.6 0.0 copy-start
  0.6 0.0 copy-start.3
  0.7 0.0 copy-start.2
  0.7 0.0 copy-start.1
  0.7 48.6 %gather_items.1 = (bf16[2,4,4,4,512,128]{5,4,3,2,1,0:T(8,128)(2,1)}, bf16[64,2,256,256]{3,2,1,0:T(8,128)(2,1)S(1)}, bf16[8,256,128]{2,1,0:T(8,128)(2,1)S(1)}, bf16[8,128,256]{2,1,0:T(8,128)(2,1)S(1)}) custom-call(f32[512,128]{1,0:T(8,128)} %items.1, bf16[64,2,256,256]{3,2,1,0:T(8,128)(2,1)} %ratings.1, s32[64,128,128]{2,1,0:T(8,128)} %bitcast.11, ...), custom_call_target="tpu_custom_call" | custom-call | tf_op jit(solution)/shard_map/gather_items/pallas_call | solution.py:260
  49.2 0.0 copy-done
  49.2 0.0 copy-done.3
  49.3 0.0 copy-done.2
  49.3 0.0 copy-done.1
  49.3 0.0 copy-start.4
  49.3 18.3 %tile_gradients.1 = (f32[2048,128]{1,0:T(8,128)}, bf16[64,256,128]{2,1,0:T(8,128)(2,1)S(1)}, s32[128]{0:T(128)S(1)}) custom-call(s32[2,64]{1,0:T(2,128)S(1)} %bitcast.8, s32[64]{0:T(128)S(1)} %bitcast.9, s32[64]{0:T(128)S(1)} %copy-done.3, f32[2048,128]{1,0:T(8,128)S(1)} %copy-done, bf16[8,256,128]{2,1,0:T(8,128)(2,1)S(1)} %get-tuple-element.9.user16, ...), custom_call_target="tpu_custom_call" | custom-call | tf_op jit(solution)/shard_map/tile_gradients/pallas_call | solution.py:382
  67.6 45.5 %reduce_items.1 = f32[512,128]{1,0:T(8,128)S(1)} custom-call(s32[128]{0:T(128)S(1)} %get-tuple-element.14.slots, bf16[64,256,128]{2,1,0:T(8,128)(2,1)S(1)} %get-tuple-element.15.parts), custom_call_target="tpu_custom_call" | custom-call | tf_op jit(solution)/shard_map/reduce_items/pallas_call | solution.py:582
  113.1 0.0 copy-done.4
  113.1 0.8 multiply_subtract_fusion
Async XLA Ops:
  0.6 48.6 %copy-start = (f32[2048,128]{1,0:T(8,128)S(1)}, f32[2048,128]{1,0:T(8,128)}, u32[]{:S(2)}) copy-start(f32[2048,128]{1,0:T(8,128)} %users.3) | copy-start | bytes 3145732
  0.6 48.6 %copy-start.3 = (s32[64]{0:T(128)S(1)}, s32[64]{0:T(128)}, u32[]{:S(2)}) copy-start(s32[64]{0:T(128)} %fetch_block.1) | copy-start | bytes 772
  0.7 48.6 %copy-start.2 = (s32[64,1]{0,1:T(1,128)S(1)}, s32[64,1]{0,1:T(1,128)}, u32[]{:S(2)}) copy-start(s32[64,1]{0,1:T(1,128)} %param.12) | copy-start | bytes 772
  0.7 48.6 %copy-start.1 = (s32[64,2]{0,1:T(2,128)S(1)}, s32[64,2]{0,1:T(2,128)}, u32[]{:S(2)}) copy-start(s32[64,2]{0,1:T(2,128)} %param.11) | copy-start | bytes 1540
  49.3 63.8 %copy-start.4 = (f32[512,128]{1,0:T(8,128)S(1)}, f32[512,128]{1,0:T(8,128)}, u32[]{:S(2)}) copy-start(f32[512,128]{1,0:T(8,128)} %items.1) | copy-start | bytes 786436

commit v5 on v4

--- a/solution.py
+++ b/solution.py
@@ -260,14 +260,13 @@
     return pl.pallas_call(
         gather_kernel,
         out_shape=(
-            pltpu.HBM((2, 4, 4, 4, 512, R), jnp.bfloat16),
+            pltpu.VMEM((2, 4, 4, 4, 512, R), jnp.bfloat16),
             pltpu.VMEM(ratings.shape, jnp.bfloat16),
             pltpu.VMEM((8, BS, R), jnp.bfloat16),
             pltpu.VMEM((8, R, BS), jnp.bfloat16),
         ),
         in_specs=[pl.BlockSpec(memory_space=pltpu.HBM)] * 4,
-        out_specs=[pl.BlockSpec(memory_space=pltpu.HBM)]
-        + [pl.BlockSpec(memory_space=pltpu.VMEM)] * 3,
+        out_specs=[pl.BlockSpec(memory_space=pltpu.VMEM)] * 4,
         scratch_shapes=[
             pltpu.VMEM((128, BS), jnp.bfloat16),
             pltpu.VMEM((512, R), jnp.float32),
@@ -283,7 +282,7 @@
             pltpu.SemaphoreType.DMA((GATHER_COPIES,)),
         ],
         compiler_params=pltpu.CompilerParams(
-            collective_id=0, has_side_effects=True, vmem_limit_bytes=12 << 20
+            collective_id=0, has_side_effects=True, vmem_limit_bytes=7 << 20
         ),
         name="gather_items",
     )(*[in_space(x, pltpu.HBM) for x in (items, ratings, observed, users)])
@@ -295,33 +294,24 @@
 
 def tile_kernel(
     tile_user, owner, fetch_block, users, user16, user16t, masked, fetched,
-    new_users, partial, slots, blocks, errors, grad, in_sems, out_sems,
+    new_users, partial, slots, errors, grad, out_sems,
 ):
     where = position()
 
-    def read(f):
+    def item(f):
         name = owner[f]
         at = (name >> 5, name >> 3, name >> 1)
         dy, dz, dx = [(a - w) & 3 for a, w in zip(at, where)]
-        away = ((name & 1) << 6) + (dy << 4) + (dz << 2) + dx
-        return pltpu.make_async_copy(
-            fetched.at[away * 2 + fetch_block[f]], blocks.at[f], in_sems.at[f]
-        )
+        rows = pl.ds(pl.multiple_of(fetch_block[f] * BS, BS), BS)
+        return fetched.at[name & 1, dy, dz, dx, rows]
 
     def write(b):
         rows = pl.ds(b * BS, BS)
         return pltpu.make_async_copy(grad.at[rows], new_users.at[rows], out_sems.at[b])
 
-    for f in range(2 * GROUP):
-        read(f).start()
     grad[...] = jnp.zeros_like(grad)
 
     def one(g, carry):
-        @pl.when(g + 2 < GROUPS)
-        def _():
-            for k in range(GROUP):
-                read((g + 2) * GROUP + k).start()
-
         @pl.when(g < GROUPS // 2)
         def _():
             for k in range(32):
@@ -335,12 +325,11 @@
 
         fetches = [g * GROUP + k for k in range(GROUP)]
         which = [[tile_user[t, f] for t in range(2)] for f in fetches]
-        for f in fetches:
-            pltpu.make_async_copy(fetched.at[0], blocks.at[f], in_sems.at[f]).wait()
+        blocks = [item(f) for f in fetches]
         for k, f in enumerate(fetches):
             for t in range(2):
                 predicted = lax.dot_general(
-                    user16[which[k][t]], blocks[f], (((1,), (1,)), ((), ())),
+                    user16[which[k][t]], blocks[k][...], (((1,), (1,)), ((), ())),
                     preferred_element_type=jnp.float32,
                 )
                 miss = predicted - masked[f, t].astype(jnp.float32)
@@ -353,11 +342,10 @@
                 )
             partial[f, pl.ds(0, R), :] = total[:, :R].astype(jnp.bfloat16)
             partial[f, pl.ds(R, R), :] = total[:, R:].astype(jnp.bfloat16)
-        for k, f in enumerate(fetches):
             for t in range(2):
                 rows = pl.ds(pl.multiple_of(which[k][t] * BS, BS), BS)
                 grad[rows, :] += jnp.dot(
-                    errors[k, t], blocks[f], preferred_element_type=jnp.float32
+                    errors[k, t], blocks[k][...], preferred_element_type=jnp.float32
                 )
         return carry
 
@@ -378,7 +366,7 @@
     smem, vmem, hbm = [
         pl.BlockSpec(memory_space=m) for m in (pltpu.SMEM, pltpu.VMEM, pltpu.HBM)
     ]
-    held = [in_space(x, pltpu.VMEM) for x in (users, user16, user16t, masked)]
+    held = [in_space(x, pltpu.VMEM) for x in (users, user16, user16t, masked, fetched)]
     return pl.pallas_call(
         tile_kernel,
         out_shape=(
@@ -386,18 +374,16 @@
             pltpu.VMEM((FETCHES, BS, R), jnp.bfloat16),
             jax.ShapeDtypeStruct((128,), jnp.int32),
         ),
-        in_specs=[smem, smem, smem, vmem, vmem, vmem, vmem, hbm],
+        in_specs=[smem, smem, smem, vmem, vmem, vmem, vmem, vmem],
         out_specs=[hbm, vmem, smem],
         scratch_shapes=[
-            pltpu.VMEM((FETCHES, BS, R), jnp.bfloat16),
             pltpu.VMEM((GROUP, 2, BS, BS), jnp.bfloat16),
             pltpu.VMEM(users.shape, jnp.float32),
-            pltpu.SemaphoreType.DMA((FETCHES,)),
             pltpu.SemaphoreType.DMA((8,)),
         ],
-        compiler_params=pltpu.CompilerParams(vmem_limit_bytes=14 << 20),
+        compiler_params=pltpu.CompilerParams(vmem_limit_bytes=6 << 20),
         name="tile_gradients",
-    )(tile_user, owner, fetch_block, *held, in_space(fetched, pltpu.HBM))
+    )(tile_user, owner, fetch_block, *held)
 
 
 REDUCE_COPIES = 48 + 3 * (4 + 4 + 4 + 6 + 3)
@@ -448,6 +434,8 @@
     def prepare(d3, d2):
         for p in thirds:
             fill(outgoing[p], p, 1 - core, d3, d2)
+
+    def fill_own(d3, d2):
         for p in thirds:
             fill(dense[p], p, core, d3, d2)
 
@@ -498,20 +486,21 @@
     todo = [(2, 0), (2, 2), (2, 1), (2, 3), (1, 2), (3, 1), (1, 3), (3, 2)]
     todo += [(1, 1), (3, 3), (1, 0), (3, 0), (0, 2), (0, 1), (0, 3), (0, 0)]
     ahead = 3
-    for d3, d2 in todo[:ahead]:
-        prepare(d3, d2)
+    prepare(*todo[0])
     greeted()
-    for d3, d2 in todo[:ahead]:
-        hand_over(d3, d2)
+    hand_over(*todo[0])
+    prepare(*todo[1])
+    hand_over(*todo[1])
     for n, (d3, d2) in enumerate(todo):
+        fill_own(d3, d2)
         collect(d3, d2)
         if d3 == 2:
             send_far(d2)
         elif d3 != 0:
             send_near(d2, 1 if d3 == 1 else -1)
-        if n + ahead < len(todo):
-            prepare(*todo[n + ahead])
-            hand_over(*todo[n + ahead])
+        for item in todo[2 if n == 0 else n + ahead : n + ahead + 1]:
+            prepare(*item)
+            hand_over(*item)
 
     low, high = pl.ds(0, 2), pl.ds(2, 2)
 
@@ -613,8 +602,7 @@
     packed = observed.reshape(FETCHES, 2, 64, 128).transpose(0, 2, 1, 3).reshape(FETCHES, 128, 128)
     gathered, masked, user16, user16t = gather(items, ratings, packed, users)
     new_users, partial, slots = tiles(
-        tile_user.T, owner, fetch_block, users, user16, user16t, masked,
-        gathered.reshape(256, BS, R),
+        tile_user.T, owner, fetch_block, users, user16, user16t, masked, gathered
     )
     new_items = items - LEARN_RATE * reduce_items(slots, partial)
     return (new_users, new_items)

time: 114 us -> 111 us (0.974)
  Pallas kernels: 112 us -> 109 us
    pallas_call x1, Pallas kernels: 18.3 us -> 16.4 us  [tiles(): pl.pallas_call(tile_kernel, out_shape=(pltpu.HBM(users.shape, jnp.float32...]
    pallas_call x1, Pallas kernels: 48.6 us -> 47.2 us  [gather(): pl.pallas_call(gather_kernel, out_shape=(pltpu.VMEM((2, 4, 4, 4, 512, R),...]
where the time goes in v5:
time: 111 us
  Pallas kernels  109 us (98%)
    pallas_call x1, Pallas kernels, gather(): pl.pallas_call(gather_kernel, out_shape=(pltpu.VMEM((2, 4, 4, 4, 512, R),...  47.2 us
    pallas_call x1, Pallas kernels, reduce_items(): pl.pallas_call(reduce_kernel, out_shape=jax.ShapeDtypeStruct((2 * BS, R),...  45.8 us
    pallas_call x1, Pallas kernels, tiles(): pl.pallas_call(tile_kernel, out_shape=(pltpu.HBM(users.shape, jnp.float32...  16.4 us

profile of v5, /device:TPU:0, one launch (start us, length us, event | category | flops | bytes accessed | tf_op | source)
XLA Modules:
  0.0 110.9 jit_solution(696858622321920845)
XLA Ops:
  0.6 0.0 copy-start
  0.6 0.0 copy-start.3
  0.7 0.0 copy-start.2
  0.7 0.0 copy-start.1
  0.7 47.2 %gather_items.1 = (bf16[2,4,4,4,512,128]{5,4,3,2,1,0:T(8,128)(2,1)S(1)}, bf16[64,2,256,256]{3,2,1,0:T(8,128)(2,1)S(1)}, bf16[8,256,128]{2,1,0:T(8,128)(2,1)S(1)}, bf16[8,128,256]{2,1,0:T(8,128)(2,1)S(1)}) custom-call(f32[512,128]{1,0:T(8,128)} %items.1, bf16[64,2,256,256]{3,2,1,0:T(8,128)(2,1)} %ratings.1, s32[64,128,128]{2,1,0:T(8,128)} %bitcast.9, ...), custom_call_target="tpu_custom_call" | custom-call | tf_op jit(solution)/shard_map/gather_items/pallas_call | solution.py:260
  47.8 0.0 copy-done
  47.8 0.0 copy-done.3
  47.9 0.0 copy-done.2
  47.9 0.0 copy-done.1
  47.9 0.0 copy-start.4
  47.9 16.4 %tile_gradients.1 = (f32[2048,128]{1,0:T(8,128)}, bf16[64,256,128]{2,1,0:T(8,128)(2,1)S(1)}, s32[128]{0:T(128)S(1)}) custom-call(s32[2,64]{1,0:T(2,128)S(1)} %bitcast.7, s32[64]{0:T(128)S(1)} %bitcast.8, s32[64]{0:T(128)S(1)} %copy-done.3, f32[2048,128]{1,0:T(8,128)S(1)} %copy-done, bf16[8,256,128]{2,1,0:T(8,128)(2,1)S(1)} %get-tuple-element.9.user16, ...), custom_call_target="tpu_custom_call" | custom-call | tf_op jit(solution)/shard_map/tile_gradients/pallas_call | solution.py:370
  64.3 45.8 %reduce_items.1 = f32[512,128]{1,0:T(8,128)S(1)} custom-call(s32[128]{0:T(128)S(1)} %get-tuple-element.14.slots, bf16[64,256,128]{2,1,0:T(8,128)(2,1)S(1)} %get-tuple-element.15.parts), custom_call_target="tpu_custom_call" | custom-call | tf_op jit(solution)/shard_map/reduce_items/pallas_call | solution.py:571
  110.2 0.0 copy-done.4
  110.2 0.8 multiply_subtract_fusion
Async XLA Ops:
  0.6 47.2 %copy-start = (f32[2048,128]{1,0:T(8,128)S(1)}, f32[2048,128]{1,0:T(8,128)}, u32[]{:S(2)}) copy-start(f32[2048,128]{1,0:T(8,128)} %users.3) | copy-start | bytes 3145732
  0.6 47.2 %copy-start.3 = (s32[64]{0:T(128)S(1)}, s32[64]{0:T(128)}, u32[]{:S(2)}) copy-start(s32[64]{0:T(128)} %fetch_block.1) | copy-start | bytes 772
  0.7 47.2 %copy-start.2 = (s32[64,1]{0,1:T(1,128)S(1)}, s32[64,1]{0,1:T(1,128)}, u32[]{:S(2)}) copy-start(s32[64,1]{0,1:T(1,128)} %param.12) | copy-start | bytes 772
  0.7 47.2 %copy-start.1 = (s32[64,2]{0,1:T(2,128)S(1)}, s32[64,2]{0,1:T(2,128)}, u32[]{:S(2)}) copy-start(s32[64,2]{0,1:T(2,128)} %param.11) | copy-start | bytes 1540
  47.9 62.3 %copy-start.4 = (f32[512,128]{1,0:T(8,128)S(1)}, f32[512,128]{1,0:T(8,128)}, u32[]{:S(2)}) copy-start(f32[512,128]{1,0:T(8,128)} %items.1) | copy-start | bytes 786436
